TPU v7x, 256 devices: a whole 4x4x8 slice. The times are simulated.
256 devices in a mesh: lat: 8 (over x_hi, y), lon: 32 (over x_lo, z, core).
Axes of the slice: x: 4 (x_hi: 2, x_lo: 2; x = x_hi * 2 + x_lo), y: 4, z: 8, core: 2. Of those that a mesh axis runs over, the one named last changes fastest.
Arguments:
- features: bfloat16 [8, 64, 128, 384], P('lat', 'lon'), may hold values from -6 to 6
- w_query: bfloat16 [384, 384], replicated, may hold values from -0.3125 to 0.3125
- w_key: bfloat16 [384, 384], replicated, may hold values from -0.3125 to 0.3125
- w_value: bfloat16 [384, 384], replicated, may hold values from -0.3125 to 0.3125
- w_out: bfloat16 [384, 384], replicated, may hold values from -0.3125 to 0.3125
- key_bias: bfloat16 [8, 64, 8, 128], P('lat', 'lon'), may hold values from -4 to 320
- neighbours: int32 [8, 64, 4], P('lat', 'lon'), may hold values from 0 to 511, as said below
- key_counts: int32 [8, 64, 4], P('lat', 'lon'), may hold values from 16 to 128, as said below
- grad_out: bfloat16 [8, 64, 128, 384], P('lat', 'lon'), may hold values from -6 to 6
Outputs:
- grad_features: bfloat16 [8, 64, 128, 384], P('lat', 'lon')
- grad_bias: float32 [8, 64, 8, 128], P('lat', 'lon')
- grad_wq: float32 [384, 384], replicated
- grad_wk: float32 [384, 384], replicated
- grad_wv: float32 [384, 384], replicated
- grad_wo: float32 [384, 384], replicated
Inputs may be any that keep to these rules, and one draw needn't show every extreme that they name: `neighbours`: entry 0 of each query block names that block itself; every entry names a block whose row differs by at most 1 (kept in range at the first and last rows) and whose column differs by at most 1 modulo 64; a block may be named more than once. `key_counts`: entry 0 is 128.
All inputs are finite; a program needn't handle non-finite values.
Results may differ from a plain program's by a relative error of at most 0.012.
Values may be sent and summed in bfloat16 or wider, within the bound.
A program may use at most 64 MiB of HBM per device.

v0:
```python
import math

import jax
import jax.numpy as jnp
import numpy as np
from jax import lax
from jax.experimental import pallas as pl
from jax.experimental.pallas import tpu as pltpu
from jax.sharding import PartitionSpec as P

BF = jnp.bfloat16
F32 = jnp.float32
HEADS = 8
PAIR = 4
WINDOW = 256
NT = (((1,), (1,)), ((), ()))
TN = (((0,), (0,)), ((), ()))
FAR = -1e30


def bf16_parts(value, count):
    parts = []
    for _ in range(count):
        part = float(np.asarray(value, dtype=jnp.bfloat16).astype(np.float64))
        parts.append(part)
        value = value - part
    return parts


def mm(a, b, dims=None):
    if dims is None:
        return jnp.dot(a, b, preferred_element_type=F32)
    return lax.dot_general(a, b, dims, preferred_element_type=F32)


def attend_kernel(
    neighbours, counts, ext, ext_bias, grad_out, w_query, w_kv, w_out,
    halo, own, bias_sum, weights,
    gathered, scores, grad_probs, probs_low, scores_low, scores_rest, grad_kv, attended_t, grad_query_t, acc,
):
    lat = lax.axis_index("lat")
    lon = lax.axis_index("lon")
    columns = 2 * lax.axis_size("lon")

    def local_slot(block):
        row = lax.div(block, columns) - lat + 1
        column = lax.rem(lax.rem(block, columns) - 2 * lon + 1 + columns, columns)
        return column * 3 + row

    slots, chans = ext.shape[1:]
    width = chans // HEADS
    entries = counts.shape[0] // 2
    keys_all = entries * slots
    root = math.sqrt(width)
    parts = bf16_parts(root, 3)
    log2e = math.log2(math.e) / root
    lane = lax.broadcasted_iota(jnp.int32, (slots, WINDOW), 1)
    row = lax.broadcasted_iota(jnp.int32, (slots, WINDOW), 0)
    place_row = lax.broadcasted_iota(jnp.int32, (HEADS, WINDOW), 0)
    place_lane = lax.broadcasted_iota(jnp.int32, (HEADS, WINDOW), 1)
    pick_row = lax.broadcasted_iota(jnp.int32, (2 * HEADS, PAIR * slots), 0)
    pick_lane = lax.broadcasted_iota(jnp.int32, (2 * HEADS, PAIR * slots), 1)
    acc[...] = jnp.zeros_like(acc)
    bias_sum[...] = jnp.zeros_like(bias_sum)
    for b in range(2):
        picks = [local_slot(neighbours[b * entries + e]) for e in range(entries)]
        feat = ext[3 * (1 + b) + 1]
        grad_rows = grad_out[b]
        query = mm(feat, w_query[...]).astype(BF)
        grad_att = mm(grad_rows, w_out[...], NT).astype(BF)
        for e in range(entries):
            gathered[b, e * slots:(e + 1) * slots, :] = ext[picks[e]]
        kv = mm(gathered[b], w_kv[...]).astype(BF)
        bias_row = jnp.concatenate([ext_bias[picks[e]] for e in range(entries)], axis=1)
        bias_rows = jnp.zeros((2 * HEADS, keys_all), F32)
        for w in range(2):
            lo = w * (chans - WINDOW)
            first = PAIR * w
            spare = PAIR * width if w == 0 else 0
            region = (lane < PAIR * width) if w == 0 else (lane >= WINDOW - PAIR * width)
            place = jnp.zeros((HEADS, WINDOW), F32)
            for hh in range(PAIR):
                start = spare + 3 * hh
                place = jnp.where(
                    (place_row == first + hh) & (place_lane >= start) & (place_lane < start + 3), 1.0, place
                )
            bias_cols = mm(bias_row, place, TN)
            key_aug = []
            for e in range(entries):
                cols = bias_cols[e * slots:(e + 1) * slots]
                cols = jnp.where((lane == spare + 3 * PAIR) & (row >= counts[b * entries + e]), FAR, cols)
                piece = kv[e * slots:(e + 1) * slots, lo:lo + WINDOW]
                key_aug.append(jnp.where(region, piece.astype(F32), cols).astype(BF))
            key_aug = jnp.concatenate(key_aug, axis=0)
            value_win = kv[:, chans + lo:chans + lo + WINDOW]
            query_win = query[:, lo:lo + WINDOW].astype(F32)
            grad_win = grad_att[:, lo:lo + WINDOW].astype(F32)
            query_aug, grad_aug = [], []
            for hh in range(PAIR):
                inside = (lane >= (first + hh) * width - lo) & (lane < (first + hh + 1) * width - lo)
                const = jnp.where(lane == spare + 3 * PAIR, 1.0, 0.0)
                for t in range(3):
                    const = jnp.where(lane == spare + 3 * hh + t, parts[t], const)
                query_aug.append(jnp.where(inside, query_win, const).astype(BF))
                grad_aug.append(jnp.where(inside, grad_win, 0.0).astype(BF))
            query_aug = jnp.concatenate(query_aug, axis=0)
            grad_aug = jnp.concatenate(grad_aug, axis=0)
            scores[...] = mm(key_aug, query_aug, NT)
            grad_probs[...] = mm(value_win, grad_aug, NT)
            for hh in range(PAIR):
                cut = pl.ds(hh * slots, slots)
                logits = scores[:, cut]
                powers = jnp.exp2((logits - jnp.max(logits, axis=0, keepdims=True)) * log2e)
                probs = powers * (1.0 / jnp.sum(powers, axis=0, keepdims=True))
                probs_low[:, cut] = probs.astype(BF)
                grads = grad_probs[:, cut]
                centre = jnp.sum(probs * grads, axis=0, keepdims=True)
                full = probs * (grads - centre)
                high = full.astype(BF)
                scores_low[:, cut] = high
                scores_rest[:, cut] = (full - high.astype(F32)).astype(BF)
            value_grad = mm(probs_low[...], grad_aug)
            key_grad = mm(scores_low[...], query_aug)
            chosen = jnp.where(pick_lane // slots + first == pick_row, 1.0, 0.0).astype(BF)
            bias_rows = bias_rows + mm(chosen, scores_low[...], NT) + mm(chosen, scores_rest[...], NT)
            scale = 1.0 / root
            base = b * keys_all
            rows = pl.ds(base, keys_all)
            half = WINDOW // 2
            edge = PAIR * width - half
            low_lane = lane[0:1, 0:half]
            if w == 0:
                grad_kv[rows, 0:half] = (key_grad[:, 0:half] * scale).astype(BF)
                grad_kv[rows, chans:chans + half] = value_grad[:, 0:half].astype(BF)
                saved_key, saved_value = key_grad[:, half:], value_grad[:, half:]
            else:
                middle = jnp.where(low_lane < edge, saved_key, key_grad[:, 0:half]) * scale
                grad_kv[rows, half:2 * half] = middle.astype(BF)
                grad_kv[rows, 2 * half:3 * half] = (key_grad[:, half:] * scale).astype(BF)
                middle = saved_value + value_grad[:, 0:half]
                grad_kv[rows, chans + half:chans + 2 * half] = middle.astype(BF)
                grad_kv[rows, chans + 2 * half:chans + 3 * half] = value_grad[:, half:].astype(BF)
            for pair in range(2):
                head = first + 2 * pair
                cut = pl.ds(2 * pair * slots, 2 * slots)
                value_rows = kv[:, chans + head * width:chans + (head + 2) * width]
                key_rows = kv[:, head * width:(head + 2) * width]
                both = mm(value_rows, probs_low[:, cut], TN)
                attended_t[head * width:(head + 1) * width, b * slots:(b + 1) * slots] = both[:width, :slots].astype(BF)
                attended_t[(head + 1) * width:(head + 2) * width, b * slots:(b + 1) * slots] = both[width:, slots:].astype(BF)
                both = mm(key_rows, scores_low[:, cut], TN) * scale
                grad_query_t[head * width:(head + 1) * width, b * slots:(b + 1) * slots] = both[:width, :slots].astype(BF)
                grad_query_t[(head + 1) * width:(head + 2) * width, b * slots:(b + 1) * slots] = both[width:, slots:].astype(BF)
        for e in range(entries):
            bias_sum[picks[e]] += bias_rows[:HEADS, e * slots:(e + 1) * slots]
        grad_feat = mm(grad_kv[pl.ds(b * keys_all, keys_all), :], w_kv[...], NT)
        for e in range(entries):
            acc[picks[e]] += grad_feat[e * slots:(e + 1) * slots]
    grad_query = jnp.transpose(grad_query_t[...].astype(F32)).astype(BF)
    feat_both = jnp.concatenate([ext[4], ext[7]], axis=0)
    query_part = mm(grad_query, w_query[...], NT)
    own[0] = acc[4] + query_part[:slots]
    own[1] = acc[7] + query_part[slots:]
    halo[...] = acc[...].astype(BF)
    grad_both = grad_out[...].reshape(2 * slots, chans)
    weights[0:chans, :] = mm(feat_both, grad_query, TN).astype(BF)
    feat_all = gathered[...].reshape(2 * keys_all, chans)
    weight_kv = mm(feat_all, grad_kv[...], TN)
    weights[chans:2 * chans, :] = weight_kv[:, :chans].astype(BF)
    weights[2 * chans:3 * chans, :] = weight_kv[:, chans:].astype(BF)
    weights[3 * chans:, :] = mm(attended_t[...], grad_both).astype(BF)


def attend_call(ids, counts, ext, ext_bias, grad_out, w_query, w_kv, w_out):
    blocks, slots, chans = ext.shape
    keys_all = ids.shape[0] // 2 * slots
    vmem = pl.BlockSpec(memory_space=pltpu.VMEM)
    smem = pl.BlockSpec(memory_space=pltpu.SMEM)
    return pl.pallas_call(
        attend_kernel,
        out_shape=[
            jax.ShapeDtypeStruct((blocks, slots, chans), BF),
            jax.ShapeDtypeStruct((2, slots, chans), F32),
            jax.ShapeDtypeStruct((blocks, HEADS, slots), F32),
            jax.ShapeDtypeStruct((4 * chans, chans), BF),
        ],
        in_specs=[smem, smem] + [vmem] * 6,
        out_specs=[vmem] * 4,
        scratch_shapes=[
            pltpu.VMEM((2, keys_all, chans), BF),
            pltpu.VMEM((keys_all, PAIR * slots), F32),
            pltpu.VMEM((keys_all, PAIR * slots), F32),
            pltpu.VMEM((keys_all, PAIR * slots), BF),
            pltpu.VMEM((keys_all, PAIR * slots), BF),
            pltpu.VMEM((keys_all, PAIR * slots), BF),
            pltpu.VMEM((2 * keys_all, 2 * chans), BF),
            pltpu.VMEM((chans, 2 * slots), BF),
            pltpu.VMEM((chans, 2 * slots), BF),
            pltpu.VMEM((blocks, slots, chans), F32),
        ],
        compiler_params=pltpu.CompilerParams(vmem_limit_bytes=48 << 20),
        name="attend_backward",
    )(ids, counts, ext, ext_bias, grad_out, w_query, w_kv, w_out)


MESH = pl.DeviceIdType.MESH
NXY = 16
NZ = 8
NPEER = NXY + NZ
ROWS = 32


def remote(src, dst, send_sem, recv_sem, device):
    return pltpu.make_async_remote_copy(
        src_ref=src, dst_ref=dst, send_sem=send_sem, recv_sem=recv_sem,
        device_id=device, device_id_type=MESH,
    )


def reduce_kernel(
    part, halo, own, bias_sum, out, grad_feat, grad_bias, from_core, half, from_first, mine, from_second, total,
    core_send, core_recv, first_send, first_recv, second_send, second_recv,
    third_send, third_recv, fourth_send, fourth_recv,
    side, side_bias, rows_out, rows_bias, edge, edge_bias,
    side_send, side_recv, edge_send, edge_recv,
):
    lat = lax.axis_index("lat")
    lon = lax.axis_index("lon")
    core = lon % 2
    z = (lon // 2) % NZ
    x_lo = lon // (2 * NZ)
    x_hi = lat // 4
    y = lat % 4
    xy = (x_hi * 2 + x_lo) * 4 + y
    partner = (lat, lon + 1 - 2 * core)
    nlat = lax.axis_size("lat")
    nlon = lax.axis_size("lon")
    east = (lat, (lon + 1) % nlon)
    west = (lat, (lon + nlon - 1) % nlon)
    north = (lat - 1, lon)
    south = (lat + 1, lon)
    base = core * NPEER
    other = (1 - core) * NPEER

    def plane_peer(index):
        x = index // 4
        return ((x // 2) * 4 + index % 4, (x % 2) * (2 * NZ) + z * 2 + core)

    def depth_peer(index):
        return (lat, x_lo * (2 * NZ) + index * 2 + core)

    barrier = pltpu.get_barrier_semaphore()
    def greet(device):
        pl.semaphore_signal(barrier, inc=1, device_id=device, device_id_type=MESH)

    greet(east)
    greet(west)
    pl.when(lat > 0)(lambda: greet(north))
    pl.when(lat < nlat - 1)(lambda: greet(south))
    @pl.loop(1, NXY)
    def _(step):
        pl.semaphore_signal(barrier, inc=1, device_id=plane_peer((xy + step) % NXY), device_id_type=MESH)

    @pl.loop(1, NZ)
    def _(step):
        pl.semaphore_signal(barrier, inc=1, device_id=depth_peer((z + step) % NZ), device_id_type=MESH)

    inner = jnp.minimum(lat, 1) + jnp.minimum(nlat - 1 - lat, 1)
    pl.semaphore_wait(barrier, NPEER + inner)

    def side_copies(index):
        device = (west, east)[index]
        source = pl.ds(9 * index, 3)
        return (
            remote(halo.at[source], side.at[1 - index], side_send.at[2 * index], side_recv.at[2 - 2 * index], device),
            remote(bias_sum.at[source], side_bias.at[1 - index], side_send.at[2 * index + 1], side_recv.at[3 - 2 * index], device),
        )

    def edge_copies(index):
        device = (north, south)[index]
        return (
            remote(rows_out.at[index], edge.at[1 - index], edge_send.at[2 * index], edge_recv.at[2 - 2 * index], device),
            remote(rows_bias.at[index], edge_bias.at[1 - index], edge_send.at[2 * index + 1], edge_recv.at[3 - 2 * index], device),
        )

    def each(copies, what):
        for copy in copies:
            getattr(copy, what)()

    def chunks(step):
        return ((xy + 2 * step + 1) % NXY, (xy + 2 * step + 2) % NXY, NXY + (z + step + 1) % NZ)

    def core_copy(chunk):
        return remote(part.at[other + chunk], from_core.at[chunk], core_send.at[chunk], core_recv.at[chunk], partner)

    def first_copy(chunk, device, slot):
        return remote(half.at[chunk], from_first.at[slot], first_send.at[chunk], first_recv.at[slot], device)

    @pl.loop(0, NZ)
    def _(step):
        for chunk in chunks(step):
            core_copy(chunk).start()

    each(side_copies(0), "start")
    each(side_copies(1), "start")

    @pl.loop(0, NZ)
    def _(step):
        a, b, c = chunks(step)
        for chunk in (a, b, c):
            core_copy(chunk).wait_recv()
            half[chunk] = (part[base + chunk].astype(jnp.float32) + from_core[chunk].astype(jnp.float32)).astype(jnp.bfloat16)
        first_copy(a, plane_peer(a), xy).start()

        @pl.when(step < NZ - 1)
        def _():
            first_copy(b, plane_peer(b), xy).start()
            first_copy(c, depth_peer(c - NXY), NXY + z).start()

    each(side_copies(0), "wait_recv")
    each(side_copies(1), "wait_recv")
    for index in range(2):
        for j in range(2):
            slot = 3 * j + 3 + 2 * index
            rows_out[index, j] = (halo[slot].astype(F32) + side[j, 2 * index].astype(F32)).astype(BF)
            rows_bias[index, j] = bias_sum[slot] + side_bias[j, 2 * index]
    pl.when(lat > 0)(lambda: each(edge_copies(0), "start"))
    pl.when(lat < nlat - 1)(lambda: each(edge_copies(1), "start"))

    from_first[xy] = half[xy]
    from_first[NXY + z] = half[NXY + z]

    def wait_first(step, index):
        slot = index
        first_copy(slot, partner, slot).wait_recv()

    @pl.loop(1, NZ)
    def _(step):
        wait_first(step, NXY + (z - step + NZ) % NZ)

    mine[1] = jnp.sum(from_first[NXY:NPEER].astype(jnp.float32), axis=0).astype(jnp.bfloat16)

    def second_b(index):
        return remote(mine.at[1], from_second.at[xy], second_send.at[index], second_recv.at[xy], plane_peer(index))

    def second_a(index):
        return remote(mine.at[0], from_second.at[NXY + z], second_send.at[NXY + index], second_recv.at[NXY + z], depth_peer(index))

    @pl.loop(1, NXY)
    def _(step):
        second_b((xy + step) % NXY).start()

    @pl.loop(1, NXY)
    def _(step):
        wait_first(step, (xy - step + NXY) % NXY)

    mine[0] = jnp.sum(from_first[0:NXY].astype(jnp.float32), axis=0).astype(jnp.bfloat16)

    @pl.loop(1, NZ)
    def _(step):
        second_a((z + step) % NZ).start()

    from_second[xy] = mine[1]
    from_second[NXY + z] = mine[0]

    def wait_second(slot):
        remote(mine.at[0], from_second.at[slot], second_send.at[slot], second_recv.at[slot], partner).wait_recv()

    def third_copy(which, slot, index, device):
        return remote(total.at[which], out.at[slot], third_send.at[index], third_recv.at[slot], device)

    def fourth_copy(slot):
        return remote(out.at[slot], out.at[slot], fourth_send.at[slot], fourth_recv.at[slot], partner)

    @pl.loop(1, NXY)
    def _(step):
        wait_second((xy - step + NXY) % NXY)

    total[1] = jnp.sum(from_second[0:NXY].astype(jnp.float32), axis=0).astype(jnp.bfloat16)

    @pl.loop(1, NZ)
    def _(step):
        index = (z + step) % NZ
        third_copy(1, base + NXY + z, NXY + index, depth_peer(index)).start()

    out[base + NXY + z] = total[1]
    fourth_copy(base + NXY + z).start()

    @pl.loop(1, NZ)
    def _(step):
        wait_second(NXY + (z - step + NZ) % NZ)

    total[0] = jnp.sum(from_second[NXY:NPEER].astype(jnp.float32), axis=0).astype(jnp.bfloat16)

    @pl.loop(1, NXY)
    def _(step):
        index = (xy + step) % NXY
        third_copy(0, base + xy, index, plane_peer(index)).start()

    out[base + xy] = total[0]
    fourth_copy(base + xy).start()

    def forward(slot):
        third_copy(0, slot, 0, partner).wait_recv()
        fourth_copy(slot).start()

    @pl.loop(1, NZ)
    def _(step):
        forward(base + NXY + (z - step + NZ) % NZ)

    @pl.loop(1, NXY)
    def _(step):
        forward(base + (xy - step + NXY) % NXY)

    @pl.loop(0, NPEER)
    def _(chunk):
        core_copy(chunk).wait_send()
        fourth_copy(base + chunk).wait_send()
        fourth_copy(other + chunk).wait_recv()

    @pl.loop(1, NXY)
    def _(step):
        index = (xy + step) % NXY
        first_copy(index, partner, index).wait_send()
        second_b(index).wait_send()
        third_copy(0, base + xy, index, partner).wait_send()

    @pl.loop(1, NZ)
    def _(step):
        index = (z + step) % NZ
        first_copy(NXY + index, partner, index).wait_send()
        second_a(index).wait_send()
        third_copy(1, base + xy, NXY + index, partner).wait_send()

    each(side_copies(0), "wait_send")
    each(side_copies(1), "wait_send")

    @pl.when(lat == 0)
    def _():
        edge[0] = jnp.zeros_like(edge[0])
        edge_bias[0] = jnp.zeros_like(edge_bias[0])

    @pl.when(lat == nlat - 1)
    def _():
        edge[1] = jnp.zeros_like(edge[1])
        edge_bias[1] = jnp.zeros_like(edge_bias[1])

    @pl.when(lat > 0)
    def _():
        each(edge_copies(0), "wait_send")
        each(edge_copies(1), "wait_recv")

    @pl.when(lat < nlat - 1)
    def _():
        each(edge_copies(1), "wait_send")
        each(edge_copies(0), "wait_recv")

    for j in range(2):
        total_grad = own[j] + side[j, 1].astype(F32) + (edge[0, j].astype(F32) + edge[1, j].astype(F32))
        grad_feat[j] = total_grad.astype(BF)
        grad_bias[j] = bias_sum[3 * j + 4] + side_bias[j, 1] + (edge_bias[0, j] + edge_bias[1, j])


def reduce_call(part, halo, own, bias_sum):
    chans = part.shape[2]
    slots = own.shape[1]
    heads = bias_sum.shape[1]
    vmem = pl.BlockSpec(memory_space=pltpu.VMEM)
    low = lambda count: pltpu.VMEM((count, ROWS, chans), BF)
    dma = pltpu.SemaphoreType.DMA
    return pl.pallas_call(
        reduce_kernel,
        out_shape=[
            jax.ShapeDtypeStruct(part.shape, BF),
            jax.ShapeDtypeStruct((2, slots, chans), BF),
            jax.ShapeDtypeStruct((2, heads, slots), F32),
        ],
        in_specs=[vmem] * 4,
        out_specs=[vmem] * 3,
        scratch_shapes=[low(NPEER), low(NPEER), low(NPEER), low(2), low(NPEER), low(2)]
        + [dma((NPEER,))] * 7 + [dma((2 * NPEER,)), dma((2 * NPEER,)), dma((2 * NPEER,))]
        + [
            pltpu.VMEM((2, 3, slots, chans), BF),
            pltpu.VMEM((2, 3, heads, slots), F32),
            pltpu.VMEM((2, 2, slots, chans), BF),
            pltpu.VMEM((2, 2, heads, slots), F32),
            pltpu.VMEM((2, 2, slots, chans), BF),
            pltpu.VMEM((2, 2, heads, slots), F32),
        ]
        + [dma((4,))] * 4,
        compiler_params=pltpu.CompilerParams(collective_id=0, has_side_effects=True, vmem_limit_bytes=32 << 20),
        name="sum_gradients",
    )(part, halo, own, bias_sum)


def halo_kernel(feat, bias, ext, ext_bias, wide_send, wide_recv, bias_send, bias_recv):
    lat = lax.axis_index("lat")
    lon = lax.axis_index("lon")
    nlat = lax.axis_size("lat")
    nlon = lax.axis_size("lon")
    core = lon % 2
    east = (lat, (lon + 1) % nlon)
    west = (lat, (lon + nlon - 1) % nlon)
    north = (lat - 1, lon)
    south = (lat + 1, lon)
    barrier = pltpu.get_barrier_semaphore()

    def greet(device):
        pl.semaphore_signal(barrier, inc=1, device_id=device, device_id_type=MESH)

    greet(east)
    greet(west)
    pl.when(lat > 0)(lambda: greet(north))
    pl.when(lat < nlat - 1)(lambda: greet(south))
    for j in range(2):
        ext[3 * j + 4] = feat[j]
        ext_bias[3 * j + 4] = bias[j].astype(F32)
    inner = jnp.minimum(lat, 1) + jnp.minimum(nlat - 1 - lat, 1)
    pl.semaphore_wait(barrier, 2 + inner)

    def copies(source, target, order, device):
        return (
            remote(ext.at[source], ext.at[target], wide_send.at[order], wide_recv.at[target], device),
            remote(ext_bias.at[source], ext_bias.at[target], bias_send.at[order], bias_recv.at[target], device),
        )

    def start(*args):
        for copy in copies(*args):
            copy.start()

    def wait_recv(slot):
        for copy in copies(slot, slot, 0, east):
            copy.wait_recv()

    def wait_send(order):
        for copy in copies(4, 4, order, east):
            copy.wait_send()

    first = 4 + 3 * core
    second = 7 - 3 * core

    def to_north():
        start(first, first + 1, 0, north)
        start(second, second + 1, 1, north)

    def to_south():
        start(first, first - 1, 2, south)
        start(second, second - 1, 3, south)

    pl.when(lat > 0)(to_north)
    pl.when(lat < nlat - 1)(to_south)
    start(7, 1, 4, east)
    start(4, 10, 5, west)

    def pass_on(row, order):
        def send_west():
            wait_recv(3 + row)
            start(3 + row, 9 + row, order, west)

        def send_east():
            wait_recv(6 + row)
            start(6 + row, row, order + 1, east)

        @pl.when(core == 0)
        def _():
            send_west()
            send_east()

        @pl.when(core == 1)
        def _():
            send_east()
            send_west()

    pl.when(lat < nlat - 1)(lambda: pass_on(2, 6))
    pl.when(lat > 0)(lambda: pass_on(0, 8))
    wait_recv(1)
    wait_recv(10)
    wait_send(4)
    wait_send(5)

    @pl.when(lat > 0)
    def _():
        wait_recv(0)
        wait_recv(9)
        for order in (0, 1, 8, 9):
            wait_send(order)

    @pl.when(lat < nlat - 1)
    def _():
        wait_recv(2)
        wait_recv(11)
        for order in (2, 3, 6, 7):
            wait_send(order)


def halo_call(feat, bias):
    _, slots, chans = feat.shape
    heads = bias.shape[1]
    vmem = pl.BlockSpec(memory_space=pltpu.VMEM)
    dma = pltpu.SemaphoreType.DMA
    return pl.pallas_call(
        halo_kernel,
        out_shape=[
            jax.ShapeDtypeStruct((12, slots, chans), BF),
            jax.ShapeDtypeStruct((12, heads, slots), F32),
        ],
        in_specs=[vmem] * 2,
        out_specs=[vmem] * 2,
        scratch_shapes=[dma((10,)), dma((12,)), dma((10,)), dma((12,))],
        compiler_params=pltpu.CompilerParams(collective_id=1, has_side_effects=True, vmem_limit_bytes=16 << 20),
        name="gather_halo",
    )(feat, bias)


def per_device(
    features, w_query, w_key, w_value, w_out, key_bias, neighbours, key_counts, grad_out
):
    brows, bcols, slots, chans = features.shape
    heads = key_bias.shape[2]
    ext, ext_bias = halo_call(features[0], key_bias[0])
    halo, own, bias_sum, weights = attend_call(
        neighbours.reshape(-1), key_counts.reshape(-1), ext, ext_bias, grad_out[0],
        w_query, jnp.concatenate([w_key, w_value], axis=1), w_out,
    )
    low, grad_features, grad_bias = reduce_call(
        weights.reshape(2 * NPEER, ROWS, chans), halo, own, bias_sum
    )
    cells = lax.axis_size("lat") * lax.axis_size("lon") * brows * bcols * slots
    summed = low.astype(F32).reshape(4, chans, chans) * float(cells) ** (-0.5)
    return (
        grad_features.reshape(brows, bcols, slots, chans),
        grad_bias.reshape(brows, bcols, heads, slots),
        summed[0],
        summed[1],
        summed[2],
        summed[3],
    )


def solution(mesh):
    placed = (
        P("lat", "lon", None, None),
        P(),
        P(),
        P(),
        P(),
        P("lat", "lon", None, None),
        P("lat", "lon", None),
        P("lat", "lon", None),
        P("lat", "lon", None, None),
    )
    return jax.shard_map(
        per_device,
        mesh=mesh,
        in_specs=placed,
        out_specs=(P("lat", "lon", None, None), P("lat", "lon", None, None), P(), P(), P(), P()),
        check_vma=False,
    )
```

profile of v0, /device:TPU:1, one launch (start us, length us, event | category | flops | bytes accessed | tf_op | source)
XLA Modules:
  0.0 76.1 jit_solution(10428778209117944784)
XLA Ops:
  0.6 0.0 copy-start.2
  0.6 0.0 copy-start.4
  0.7 0.0 copy-start.1
  0.7 0.0 copy-start
  0.7 0.0 copy-start.3
  0.7 0.8 %reshape.38.neighbours = s32[8]{0:T(128)S(1)} reshape(s32[1,2,4]{2,1,0:T(2,128)} %param.15) | data formatting | bytes 64 | tf_op jit(solution)/shard_map/reshape | solution.py:622
  1.5 0.8 reshape.39.counts
  2.3 1.1 %pad_maximum_fusion.w_kv = bf16[384,768]{1,0:T(8,128)(2,1)S(1)} fusion(bf16[384,384]{1,0:T(8,128)(2,1)} %param.12, bf16[384,384]{1,0:T(8,128)(2,1)} %param.11), kind=kLoop, calls=%fused_computation.1 | loop fusion | flops 1179648 | bytes 1179648 | tf_op jit(solution)/shard_map/concatenate | solution.py:623
  3.4 0.0 copy-done.4
  3.4 0.0 copy-done.3
  3.4 14.4 %gather_halo.1 = (bf16[12,128,384]{2,1,0:T(8,128)(2,1)S(1)}, f32[12,8,128]{2,1,0:T(8,128)S(1)}) custom-call(bf16[2,128,384]{2,1,0:T(8,128)(2,1)S(1)} %bitcast.12, bf16[2,8,128]{2,1,0:T(8,128)(2,1)S(1)} %bitcast.15), custom_call_target="tpu_custom_call" | custom-call | tf_op jit(solution)/shard_map/gather_halo/pallas_call | solution.py:601
  17.8 0.0 copy-done.2
  17.8 0.0 copy-done.1
  17.8 0.0 copy-done
  17.8 10.8 %attend_backward.1 = (bf16[12,128,384]{2,1,0:T(8,128)(2,1)S(1)}, f32[2,128,384]{2,1,0:T(8,128)S(1)}, f32[12,8,128]{2,1,0:T(8,128)S(1)}, bf16[1536,384]{1,0:T(8,128)(2,1)S(1)}) custom-call(s32[8]{0:T(128)S(1)} %reshape.38.neighbours, s32[8]{0:T(128)S(1)} %reshape.39.counts, bf16[12,128,384]{2,1,0:T(8,128)(2,1)S(1)} %get-tuple-element.15.ext, ...), custom_call_target="tpu_custom_call" | custom-call | tf_op jit(solution)/shard_map/attend_backward/pallas_call | solution.py:179
  28.6 44.5 %sum_gradients.1 = (bf16[48,32,384]{2,1,0:T(8,128)(2,1)S(1)}, bf16[2,128,384]{2,1,0:T(8,128)(2,1)S(1)}, f32[2,8,128]{2,1,0:T(8,128)S(1)}) custom-call(bf16[48,32,384]{2,1,0:T(8,128)(2,1)S(1)} %bitcast.10, bf16[12,128,384]{2,1,0:T(8,128)(2,1)S(1)} %get-tuple-element.18.halo, f32[2,128,384]{2,1,0:T(8,128)S(1)} %get-tuple-element.19.own, ...), custom_call_target="tpu_custom_call" | custom-call | tf_op jit(solution)/shard_map/sum_gradients/pallas_call | solution.py:471
  73.1 0.3 convert_multiply_fusion
  73.4 1.4 %fusion = (f32[12,32,384]{2,1,0:T(8,128)}, f32[12,32,384]{2,1,0:T(8,128)}, f32[12,32,384]{2,1,0:T(8,128)}, f32[12,32,384]{2,1,0:T(8,128)}) fusion(f32[48,32,384]{2,1,0:T(8,128)S(1)} %convert_multiply_fusion), kind=kLoop, calls=%fused_computation.2 | loop fusion | bytes 4718592 | tf_op jit(solution)/shard_map/slice | solution.py:636
  74.8 0.7 copy.17
  75.5 0.6 copy.18
Async XLA Ops:
  0.6 17.2 %copy-start.2 = (bf16[1,2,128,384]{3,2,1,0:T(8,128)(2,1)S(1)}, bf16[1,2,128,384]{3,2,1,0:T(8,128)(2,1)}, u32[]{:S(2)}) copy-start(bf16[1,2,128,384]{3,2,1,0:T(8,128)(2,1)} %param.17) | copy-start | bytes 589828
  0.6 2.7 %copy-start.4 = (bf16[1,2,8,128]{3,2,1,0:T(8,128)(2,1)S(1)}, bf16[1,2,8,128]{3,2,1,0:T(8,128)(2,1)}, u32[]{:S(2)}) copy-start(bf16[1,2,8,128]{3,2,1,0:T(8,128)(2,1)} %param.14) | copy-start | bytes 12292
  0.7 17.2 %copy-start.1 = (bf16[384,384]{1,0:T(8,128)(2,1)S(1)}, bf16[384,384]{1,0:T(8,128)(2,1)}, u32[]{:S(2)}) copy-start(bf16[384,384]{1,0:T(8,128)(2,1)} %w_out.1) | copy-start | bytes 884740
  0.7 17.2 %copy-start = (bf16[384,384]{1,0:T(8,128)(2,1)S(1)}, bf16[384,384]{1,0:T(8,128)(2,1)}, u32[]{:S(2)}) copy-start(bf16[384,384]{1,0:T(8,128)(2,1)} %w_query.1) | copy-start | bytes 884740
  0.7 2.7 %copy-start.3 = (bf16[1,2,128,384]{3,2,1,0:T(8,128)(2,1)S(1)}, bf16[1,2,128,384]{3,2,1,0:T(8,128)(2,1)}, u32[]{:S(2)}) copy-start(bf16[1,2,128,384]{3,2,1,0:T(8,128)(2,1)} %param.9) | copy-start | bytes 589828
where the time goes:
time: 76.2 us; the launch traced here: 76.1 us
  Pallas kernels  69.6 us (91%)
  local copies, waits for them, and re-layouts  4.34 us (6%)
  other arithmetic  1.39 us (2%)
    pallas_call x1, Pallas kernels, reduce_call(): pl.pallas_call(reduce_kernel, out_shape=[jax.ShapeDtypeStruct(part.shape,...  44.5 us
    pallas_call x1, Pallas kernels, halo_call(): pl.pallas_call(halo_kernel, out_shape=[jax.ShapeDtypeStruct((12, slots, c...  14.4 us
    pallas_call x1, Pallas kernels, attend_call(): pl.pallas_call(attend_kernel, out_shape=[jax.ShapeDtypeStruct((blocks, sl...  10.8 us

commit v1 on v0

--- a/solution.py
+++ b/solution.py
@@ -33,10 +33,10 @@
     return lax.dot_general(a, b, dims, preferred_element_type=F32)
 
 
-def attend_kernel(
-    neighbours, counts, ext, ext_bias, grad_out, w_query, w_kv, w_out,
-    halo, own, bias_sum, weights,
-    gathered, scores, grad_probs, probs_low, scores_low, scores_rest, grad_kv, attended_t, grad_query_t, acc,
+def attend(
+    neighbours, counts, ext, ext_bias, grad_out, w_query, w_key, w_value, w_out, part,
+    w_kv, gathered, scores, grad_probs, probs_low, scores_low, scores_rest, grad_kv,
+    attended_t, grad_query_t, bias_parts,
 ):
     lat = lax.axis_index("lat")
     lon = lax.axis_index("lon")
@@ -45,11 +45,11 @@
     def local_slot(block):
         row = lax.div(block, columns) - lat + 1
         column = lax.rem(lax.rem(block, columns) - 2 * lon + 1 + columns, columns)
-        return column * 3 + row
+        return jnp.clip(column, 0, 3) * 3 + jnp.clip(row, 0, 2)
 
     slots, chans = ext.shape[1:]
     width = chans // HEADS
-    entries = counts.shape[0] // 2
+    entries = counts.shape[2]
     keys_all = entries * slots
     root = math.sqrt(width)
     parts = bf16_parts(root, 3)
@@ -60,10 +60,12 @@
     place_lane = lax.broadcasted_iota(jnp.int32, (HEADS, WINDOW), 1)
     pick_row = lax.broadcasted_iota(jnp.int32, (2 * HEADS, PAIR * slots), 0)
     pick_lane = lax.broadcasted_iota(jnp.int32, (2 * HEADS, PAIR * slots), 1)
-    acc[...] = jnp.zeros_like(acc)
-    bias_sum[...] = jnp.zeros_like(bias_sum)
+    w_kv[:, :chans] = w_key[...]
+    w_kv[:, chans:] = w_value[...]
+    all_picks = []
     for b in range(2):
-        picks = [local_slot(neighbours[b * entries + e]) for e in range(entries)]
+        picks = [local_slot(neighbours[0, b, e]) for e in range(entries)]
+        all_picks.append(picks)
         feat = ext[3 * (1 + b) + 1]
         grad_rows = grad_out[b]
         query = mm(feat, w_query[...]).astype(BF)
@@ -88,7 +90,7 @@
             key_aug = []
             for e in range(entries):
                 cols = bias_cols[e * slots:(e + 1) * slots]
-                cols = jnp.where((lane == spare + 3 * PAIR) & (row >= counts[b * entries + e]), FAR, cols)
+                cols = jnp.where((lane == spare + 3 * PAIR) & (row >= counts[0, b, e]), FAR, cols)
                 piece = kv[e * slots:(e + 1) * slots, lo:lo + WINDOW]
                 key_aug.append(jnp.where(region, piece.astype(F32), cols).astype(BF))
             key_aug = jnp.concatenate(key_aug, axis=0)
@@ -152,55 +154,49 @@
                 grad_query_t[head * width:(head + 1) * width, b * slots:(b + 1) * slots] = both[:width, :slots].astype(BF)
                 grad_query_t[(head + 1) * width:(head + 2) * width, b * slots:(b + 1) * slots] = both[width:, slots:].astype(BF)
         for e in range(entries):
-            bias_sum[picks[e]] += bias_rows[:HEADS, e * slots:(e + 1) * slots]
-        grad_feat = mm(grad_kv[pl.ds(b * keys_all, keys_all), :], w_kv[...], NT)
-        for e in range(entries):
-            acc[picks[e]] += grad_feat[e * slots:(e + 1) * slots]
+            bias_parts[b, e] = bias_rows[:HEADS, e * slots:(e + 1) * slots]
     grad_query = jnp.transpose(grad_query_t[...].astype(F32)).astype(BF)
     feat_both = jnp.concatenate([ext[4], ext[7]], axis=0)
+    grad_both = grad_out[...].reshape(2 * slots, chans)
+    piece = chans // ROWS
+
+    def put(index, value):
+        part[index * piece:(index + 1) * piece] = value.astype(BF).reshape(piece, ROWS, chans)
+
+    put(0, mm(feat_both, grad_query, TN))
+    put(3, mm(attended_t[...], grad_both))
+    weight_kv = mm(gathered[...].reshape(2 * keys_all, chans), grad_kv[...], TN)
+    put(1, weight_kv[:, :chans])
+    put(2, weight_kv[:, chans:])
+    return all_picks, grad_query
+
+
+def scatter(all_picks, grad_query, w_query, w_kv, grad_kv, bias_parts, feat_parts, halo, own, bias_sum):
+    slots, chans = halo.shape[1:]
+    entries = len(all_picks[0])
+    keys_all = entries * slots
+    for b in range(2):
+        feat_parts[b] = mm(grad_kv[pl.ds(b * keys_all, keys_all), :], w_kv[...], NT)
     query_part = mm(grad_query, w_query[...], NT)
-    own[0] = acc[4] + query_part[:slots]
-    own[1] = acc[7] + query_part[slots:]
-    halo[...] = acc[...].astype(BF)
-    grad_both = grad_out[...].reshape(2 * slots, chans)
-    weights[0:chans, :] = mm(feat_both, grad_query, TN).astype(BF)
-    feat_all = gathered[...].reshape(2 * keys_all, chans)
-    weight_kv = mm(feat_all, grad_kv[...], TN)
-    weights[chans:2 * chans, :] = weight_kv[:, :chans].astype(BF)
-    weights[2 * chans:3 * chans, :] = weight_kv[:, chans:].astype(BF)
-    weights[3 * chans:, :] = mm(attended_t[...], grad_both).astype(BF)
-
-
-def attend_call(ids, counts, ext, ext_bias, grad_out, w_query, w_kv, w_out):
-    blocks, slots, chans = ext.shape
-    keys_all = ids.shape[0] // 2 * slots
-    vmem = pl.BlockSpec(memory_space=pltpu.VMEM)
-    smem = pl.BlockSpec(memory_space=pltpu.SMEM)
-    return pl.pallas_call(
-        attend_kernel,
-        out_shape=[
-            jax.ShapeDtypeStruct((blocks, slots, chans), BF),
-            jax.ShapeDtypeStruct((2, slots, chans), F32),
-            jax.ShapeDtypeStruct((blocks, HEADS, slots), F32),
-            jax.ShapeDtypeStruct((4 * chans, chans), BF),
-        ],
-        in_specs=[smem, smem] + [vmem] * 6,
-        out_specs=[vmem] * 4,
-        scratch_shapes=[
-            pltpu.VMEM((2, keys_all, chans), BF),
-            pltpu.VMEM((keys_all, PAIR * slots), F32),
-            pltpu.VMEM((keys_all, PAIR * slots), F32),
-            pltpu.VMEM((keys_all, PAIR * slots), BF),
-            pltpu.VMEM((keys_all, PAIR * slots), BF),
-            pltpu.VMEM((keys_all, PAIR * slots), BF),
-            pltpu.VMEM((2 * keys_all, 2 * chans), BF),
-            pltpu.VMEM((chans, 2 * slots), BF),
-            pltpu.VMEM((chans, 2 * slots), BF),
-            pltpu.VMEM((blocks, slots, chans), F32),
-        ],
-        compiler_params=pltpu.CompilerParams(vmem_limit_bytes=48 << 20),
-        name="attend_backward",
-    )(ids, counts, ext, ext_bias, grad_out, w_query, w_kv, w_out)
+    for slot in range(halo.shape[0]):
+        column = slot // 3
+        total, bias_total = None, None
+        for b in range(2):
+            if column - b not in (0, 1, 2):
+                continue
+            for e in range(1, entries):
+                hit = all_picks[b][e] == slot
+                piece = jnp.where(hit, feat_parts[b, e * slots:(e + 1) * slots], 0.0)
+                total = piece if total is None else total + piece
+                piece = jnp.where(hit, bias_parts[b, e], 0.0)
+                bias_total = piece if bias_total is None else bias_total + piece
+        if slot in (4, 7):
+            b = column - 1
+            own[b] = total + (feat_parts[b, 0:slots] + query_part[b * slots:(b + 1) * slots])
+            bias_total = bias_total + bias_parts[b, 0]
+        else:
+            halo[slot] = total.astype(BF)
+        bias_sum[slot] = bias_total
 
 
 MESH = pl.DeviceIdType.MESH
@@ -217,8 +213,11 @@
     )
 
 
-def reduce_kernel(
-    part, halo, own, bias_sum, out, grad_feat, grad_bias, from_core, half, from_first, mine, from_second, total,
+def layer_kernel(
+    neighbours, counts, ext, ext_bias, grad_out, w_query, w_key, w_value, w_out,
+    out, grad_feat, grad_bias,
+    part, halo, own, bias_sum, feat_parts, bias_parts, w_kv, gathered, scores, grad_probs, probs_low,
+    scores_low, scores_rest, grad_kv, attended_t, grad_query_t, from_core, half, from_first, mine, from_second, total,
     core_send, core_recv, first_send, first_recv, second_send, second_recv,
     third_send, third_recv, fourth_send, fourth_recv,
     side, side_bias, rows_out, rows_bias, edge, edge_bias,
@@ -265,6 +264,11 @@
     def _(step):
         pl.semaphore_signal(barrier, inc=1, device_id=depth_peer((z + step) % NZ), device_id_type=MESH)
 
+    all_picks, grad_query = attend(
+        neighbours, counts, ext, ext_bias, grad_out, w_query, w_key, w_value, w_out, part,
+        w_kv, gathered, scores, grad_probs, probs_low, scores_low, scores_rest, grad_kv,
+        attended_t, grad_query_t, bias_parts,
+    )
     inner = jnp.minimum(lat, 1) + jnp.minimum(nlat - 1 - lat, 1)
     pl.semaphore_wait(barrier, NPEER + inner)
 
@@ -301,6 +305,7 @@
         for chunk in chunks(step):
             core_copy(chunk).start()
 
+    scatter(all_picks, grad_query, w_query, w_kv, grad_kv, bias_parts, feat_parts, halo, own, bias_sum)
     each(side_copies(0), "start")
     each(side_copies(1), "start")
 
@@ -461,36 +466,62 @@
         grad_bias[j] = bias_sum[3 * j + 4] + side_bias[j, 1] + (edge_bias[0, j] + edge_bias[1, j])
 
 
-def reduce_call(part, halo, own, bias_sum):
-    chans = part.shape[2]
-    slots = own.shape[1]
-    heads = bias_sum.shape[1]
+def layer_call(neighbours, counts, ext, ext_bias, grad_out, w_query, w_key, w_value, w_out):
+    blocks, slots, chans = ext.shape
+    heads = ext_bias.shape[1]
+    entries = counts.shape[2]
+    keys_all = entries * slots
     vmem = pl.BlockSpec(memory_space=pltpu.VMEM)
-    low = lambda count: pltpu.VMEM((count, ROWS, chans), BF)
+    smem = pl.BlockSpec(memory_space=pltpu.SMEM)
+    low = lambda *shape: pltpu.VMEM(shape, BF)
+    wide = lambda *shape: pltpu.VMEM(shape, F32)
     dma = pltpu.SemaphoreType.DMA
     return pl.pallas_call(
-        reduce_kernel,
+        layer_kernel,
         out_shape=[
-            jax.ShapeDtypeStruct(part.shape, BF),
+            jax.ShapeDtypeStruct((2 * NPEER, ROWS, chans), BF),
             jax.ShapeDtypeStruct((2, slots, chans), BF),
             jax.ShapeDtypeStruct((2, heads, slots), F32),
         ],
-        in_specs=[vmem] * 4,
+        in_specs=[smem] * 2 + [vmem] * 7,
         out_specs=[vmem] * 3,
-        scratch_shapes=[low(NPEER), low(NPEER), low(NPEER), low(2), low(NPEER), low(2)]
-        + [dma((NPEER,))] * 7 + [dma((2 * NPEER,)), dma((2 * NPEER,)), dma((2 * NPEER,))]
+        scratch_shapes=[
+            low(2 * NPEER, ROWS, chans),
+            low(blocks, slots, chans),
+            wide(2, slots, chans),
+            wide(blocks, heads, slots),
+            wide(2, keys_all, chans),
+            wide(2, entries, heads, slots),
+            low(chans, 2 * chans),
+            low(2, keys_all, chans),
+            wide(keys_all, PAIR * slots),
+            wide(keys_all, PAIR * slots),
+            low(keys_all, PAIR * slots),
+            low(keys_all, PAIR * slots),
+            low(keys_all, PAIR * slots),
+            low(2 * keys_all, 2 * chans),
+            low(chans, 2 * slots),
+            low(chans, 2 * slots),
+            low(NPEER, ROWS, chans),
+            low(NPEER, ROWS, chans),
+            low(NPEER, ROWS, chans),
+            low(2, ROWS, chans),
+            low(NPEER, ROWS, chans),
+            low(2, ROWS, chans),
+        ]
+        + [dma((NPEER,))] * 7 + [dma((2 * NPEER,))] * 3
         + [
-            pltpu.VMEM((2, 3, slots, chans), BF),
-            pltpu.VMEM((2, 3, heads, slots), F32),
-            pltpu.VMEM((2, 2, slots, chans), BF),
-            pltpu.VMEM((2, 2, heads, slots), F32),
-            pltpu.VMEM((2, 2, slots, chans), BF),
-            pltpu.VMEM((2, 2, heads, slots), F32),
+            low(2, 3, slots, chans),
+            wide(2, 3, heads, slots),
+            low(2, 2, slots, chans),
+            wide(2, 2, heads, slots),
+            low(2, 2, slots, chans),
+            wide(2, 2, heads, slots),
         ]
         + [dma((4,))] * 4,
-        compiler_params=pltpu.CompilerParams(collective_id=0, has_side_effects=True, vmem_limit_bytes=32 << 20),
-        name="sum_gradients",
-    )(part, halo, own, bias_sum)
+        compiler_params=pltpu.CompilerParams(collective_id=0, has_side_effects=True, vmem_limit_bytes=48 << 20),
+        name="layer_backward",
+    )(neighbours, counts, ext, ext_bias, grad_out, w_query, w_key, w_value, w_out)
 
 
 def halo_kernel(feat, bias, ext, ext_bias, wide_send, wide_recv, bias_send, bias_recv):
@@ -547,8 +578,10 @@
         start(first, first - 1, 2, south)
         start(second, second - 1, 3, south)
 
+    seam = nlat // 2
+    pl.when(lat == seam - 1)(to_south)
     pl.when(lat > 0)(to_north)
-    pl.when(lat < nlat - 1)(to_south)
+    pl.when((lat < nlat - 1) & (lat != seam - 1))(to_south)
     start(7, 1, 4, east)
     start(4, 10, 5, west)
 
@@ -571,8 +604,9 @@
             send_east()
             send_west()
 
+    pl.when(lat == seam - 1)(lambda: pass_on(0, 8))
     pl.when(lat < nlat - 1)(lambda: pass_on(2, 6))
-    pl.when(lat > 0)(lambda: pass_on(0, 8))
+    pl.when((lat > 0) & (lat != seam - 1))(lambda: pass_on(0, 8))
     wait_recv(1)
     wait_recv(10)
     wait_send(4)
@@ -618,12 +652,8 @@
     brows, bcols, slots, chans = features.shape
     heads = key_bias.shape[2]
     ext, ext_bias = halo_call(features[0], key_bias[0])
-    halo, own, bias_sum, weights = attend_call(
-        neighbours.reshape(-1), key_counts.reshape(-1), ext, ext_bias, grad_out[0],
-        w_query, jnp.concatenate([w_key, w_value], axis=1), w_out,
-    )
-    low, grad_features, grad_bias = reduce_call(
-        weights.reshape(2 * NPEER, ROWS, chans), halo, own, bias_sum
+    low, grad_features, grad_bias = layer_call(
+        neighbours, key_counts, ext, ext_bias, grad_out[0], w_query, w_key, w_value, w_out
     )
     cells = lax.axis_size("lat") * lax.axis_size("lon") * brows * bcols * slots
     summed = low.astype(F32).reshape(4, chans, chans) * float(cells) ** (-0.5)

time: 76.2 us -> 76 us (level)
  local copies, waits for them, and re-layouts: 4.34 us -> 10.4 us
  Pallas kernels: 69.6 us -> 64.2 us
  other arithmetic: 1.39 us -> 0.31 us
    unnamed x12 -> x20, local copies, waits for them, and re-layouts: 1.3 us -> 9 us
    pallas_call x2 -> x1, Pallas kernels: 55.2 us -> 50 us  [layer_call(): pl.pallas_call(layer_kernel, out_shape=[jax.ShapeDtypeStruct((2 * NPEER,...]
    reshape x2 -> x0, local copies, waits for them, and re-layouts: 1.6 us -> none  [the longest x1 0.84 us: per_device(): neighbours.reshape(-1)]
    concatenate x1 -> x0, other arithmetic: 1.1 us -> none  [per_device(): jnp.concatenate([w_key, w_value], axis=1)]
where the time goes in v1:
time: 76 us; the launch traced here: 75.6 us
  Pallas kernels  64.2 us (84%)
  local copies, waits for them, and re-layouts  10.4 us (14%)
    pallas_call x1, Pallas kernels, layer_call(): pl.pallas_call(layer_kernel, out_shape=[jax.ShapeDtypeStruct((2 * NPEER,...  50 us
    pallas_call x1, Pallas kernels, halo_call(): pl.pallas_call(halo_kernel, out_shape=[jax.ShapeDtypeStruct((12, slots, c...  14.2 us
    unnamed x20, local copies, waits for them, and re-layouts  9 us

profile of v1, /device:TPU:1, one launch (start us, length us, event | category | flops | bytes accessed | tf_op | source)
XLA Modules:
  0.0 75.6 jit_solution(6951935147719968532)
XLA Ops:
  0.6 0.0 copy-start.5
  0.6 0.9 %copy-done.5 = bf16[1,2,128,384]{3,2,1,0:T(8,128)(2,1)S(1)} copy-done((bf16[1,2,128,384]{3,2,1,0:T(8,128)(2,1)S(1)}, bf16[1,2,128,384]{3,2,1,0:T(8,128)(2,1)}, u32[]{:S(2)}) %copy-start.5) | copy-done | bytes 196632
  1.6 0.0 copy-start.6
  1.6 0.7 copy-done.6
  2.2 14.2 %gather_halo.1 = (bf16[12,128,384]{2,1,0:T(8,128)(2,1)S(1)}, f32[12,8,128]{2,1,0:T(8,128)S(1)}) custom-call(bf16[2,128,384]{2,1,0:T(8,128)(2,1)S(1)} %bitcast.10, bf16[2,8,128]{2,1,0:T(8,128)(2,1)S(1)} %bitcast.13), custom_call_target="tpu_custom_call" | custom-call | tf_op jit(solution)/shard_map/gather_halo/pallas_call | solution.py:635
  16.5 0.0 copy-start
  16.5 1.0 %copy-done = bf16[384,384]{1,0:T(8,128)(2,1)S(1)} copy-done((bf16[384,384]{1,0:T(8,128)(2,1)S(1)}, bf16[384,384]{1,0:T(8,128)(2,1)}, u32[]{:S(2)}) %copy-start) | copy-done | bytes 294936
  17.5 0.0 copy-start.1
  17.5 1.0 %copy-done.1 = bf16[384,384]{1,0:T(8,128)(2,1)S(1)} copy-done((bf16[384,384]{1,0:T(8,128)(2,1)S(1)}, bf16[384,384]{1,0:T(8,128)(2,1)}, u32[]{:S(2)}) %copy-start.1) | copy-done | bytes 294936
  18.4 0.0 copy-start.2
  18.4 1.0 %copy-done.2 = bf16[384,384]{1,0:T(8,128)(2,1)S(1)} copy-done((bf16[384,384]{1,0:T(8,128)(2,1)S(1)}, bf16[384,384]{1,0:T(8,128)(2,1)}, u32[]{:S(2)}) %copy-start.2) | copy-done | bytes 294936
  19.4 0.0 copy-start.3
  19.4 1.0 %copy-done.3 = bf16[384,384]{1,0:T(8,128)(2,1)S(1)} copy-done((bf16[384,384]{1,0:T(8,128)(2,1)S(1)}, bf16[384,384]{1,0:T(8,128)(2,1)}, u32[]{:S(2)}) %copy-start.3) | copy-done | bytes 294936
  20.3 0.0 copy-start.4
  20.3 0.9 %copy-done.4 = bf16[1,2,128,384]{3,2,1,0:T(8,128)(2,1)S(1)} copy-done((bf16[1,2,128,384]{3,2,1,0:T(8,128)(2,1)S(1)}, bf16[1,2,128,384]{3,2,1,0:T(8,128)(2,1)}, u32[]{:S(2)}) %copy-start.4) | copy-done | bytes 196632
  21.3 0.0 copy-start.7
  21.3 0.7 copy-done.7
  22.0 0.0 copy-start.8
  22.0 0.7 copy-done.8
  22.6 50.0 %layer_backward.1 = (bf16[48,32,384]{2,1,0:T(8,128)(2,1)S(1)}, bf16[2,128,384]{2,1,0:T(8,128)(2,1)S(1)}, f32[2,8,128]{2,1,0:T(8,128)S(1)}) custom-call(s32[1,2,4]{2,1,0:T(2,128)S(1)} %copy-done.7, s32[1,2,4]{2,1,0:T(2,128)S(1)} %copy-done.8, bf16[12,128,384]{2,1,0:T(8,128)(2,1)S(1)} %get-tuple-element.11.ext, f32[12,8,128]{2,1,0:T(8,128)S(1)} %get-tuple-element.12.ext_bias, ...), custom_call_target="tpu_custom_call" | custom-call | tf_op jit(solution)/shard_map/layer_backward/pallas_call | solution.py:479
  72.6 0.3 convert_multiply_fusion
  72.9 1.4 %fusion = (f32[12,32,384]{2,1,0:T(8,128)}, f32[12,32,384]{2,1,0:T(8,128)}, f32[12,32,384]{2,1,0:T(8,128)}, f32[12,32,384]{2,1,0:T(8,128)}) fusion(f32[48,32,384]{2,1,0:T(8,128)S(1)} %convert_multiply_fusion), kind=kLoop, calls=%fused_computation.1 | loop fusion | bytes 4718592 | tf_op jit(solution)/shard_map/slice | solution.py:666
  74.4 0.7 copy.17
  75.0 0.6 copy.18
Async XLA Ops:
  0.6 0.9 %copy-start.5 = (bf16[1,2,128,384]{3,2,1,0:T(8,128)(2,1)S(1)}, bf16[1,2,128,384]{3,2,1,0:T(8,128)(2,1)}, u32[]{:S(2)}) copy-start(bf16[1,2,128,384]{3,2,1,0:T(8,128)(2,1)} %param.9) | copy-start | bytes 589828
  1.6 0.7 copy-start.6
  16.5 1.0 %copy-start = (bf16[384,384]{1,0:T(8,128)(2,1)S(1)}, bf16[384,384]{1,0:T(8,128)(2,1)}, u32[]{:S(2)}) copy-start(bf16[384,384]{1,0:T(8,128)(2,1)} %w_query.1) | copy-start | bytes 884740
  17.5 1.0 %copy-start.1 = (bf16[384,384]{1,0:T(8,128)(2,1)S(1)}, bf16[384,384]{1,0:T(8,128)(2,1)}, u32[]{:S(2)}) copy-start(bf16[384,384]{1,0:T(8,128)(2,1)} %w_key.1) | copy-start | bytes 884740
  18.4 1.0 %copy-start.2 = (bf16[384,384]{1,0:T(8,128)(2,1)S(1)}, bf16[384,384]{1,0:T(8,128)(2,1)}, u32[]{:S(2)}) copy-start(bf16[384,384]{1,0:T(8,128)(2,1)} %w_value.1) | copy-start | bytes 884740
  19.4 1.0 %copy-start.3 = (bf16[384,384]{1,0:T(8,128)(2,1)S(1)}, bf16[384,384]{1,0:T(8,128)(2,1)}, u32[]{:S(2)}) copy-start(bf16[384,384]{1,0:T(8,128)(2,1)} %w_out.1) | copy-start | bytes 884740
  20.3 0.9 %copy-start.4 = (bf16[1,2,128,384]{3,2,1,0:T(8,128)(2,1)S(1)}, bf16[1,2,128,384]{3,2,1,0:T(8,128)(2,1)}, u32[]{:S(2)}) copy-start(bf16[1,2,128,384]{3,2,1,0:T(8,128)(2,1)} %param.17) | copy-start | bytes 589828
  21.3 0.7 copy-start.7
  22.0 0.7 copy-start.8

commit v2 on v1

--- a/solution.py
+++ b/solution.py
@@ -33,8 +33,18 @@
     return lax.dot_general(a, b, dims, preferred_element_type=F32)
 
 
+def project(ext, grad_rows, w_query, w_out, w_kv, query, grad_att, key_value):
+    slots = ext.shape[1]
+    entries = key_value.shape[0] // (2 * slots)
+    for b in range(2):
+        feat = ext[3 * b + 4]
+        query[b] = mm(feat, w_query[...]).astype(BF)
+        grad_att[b] = mm(grad_rows[b], w_out[...], NT).astype(BF)
+        key_value[b * entries * slots:(b * entries + 1) * slots] = mm(feat, w_kv[...]).astype(BF)
+
+
 def attend(
-    neighbours, counts, ext, ext_bias, grad_out, w_query, w_key, w_value, w_out, part,
+    neighbours, counts, ext, ext_bias, grad_out, query_all, grad_att_all, key_value, part,
     w_kv, gathered, scores, grad_probs, probs_low, scores_low, scores_rest, grad_kv,
     attended_t, grad_query_t, bias_parts,
 ):
@@ -60,19 +70,18 @@
     place_lane = lax.broadcasted_iota(jnp.int32, (HEADS, WINDOW), 1)
     pick_row = lax.broadcasted_iota(jnp.int32, (2 * HEADS, PAIR * slots), 0)
     pick_lane = lax.broadcasted_iota(jnp.int32, (2 * HEADS, PAIR * slots), 1)
-    w_kv[:, :chans] = w_key[...]
-    w_kv[:, chans:] = w_value[...]
     all_picks = []
     for b in range(2):
         picks = [local_slot(neighbours[0, b, e]) for e in range(entries)]
         all_picks.append(picks)
-        feat = ext[3 * (1 + b) + 1]
-        grad_rows = grad_out[b]
-        query = mm(feat, w_query[...]).astype(BF)
-        grad_att = mm(grad_rows, w_out[...], NT).astype(BF)
-        for e in range(entries):
+        query = query_all[b]
+        grad_att = grad_att_all[b]
+        gathered[b, 0:slots, :] = ext[3 * b + 4]
+        for e in range(1, entries):
             gathered[b, e * slots:(e + 1) * slots, :] = ext[picks[e]]
-        kv = mm(gathered[b], w_kv[...]).astype(BF)
+        rest = pl.ds(b * keys_all + slots, keys_all - slots)
+        key_value[rest, :] = mm(gathered[b, slots:], w_kv[...]).astype(BF)
+        kv = key_value[pl.ds(b * keys_all, keys_all), :]
         bias_row = jnp.concatenate([ext_bias[picks[e]] for e in range(entries)], axis=1)
         bias_rows = jnp.zeros((2 * HEADS, keys_all), F32)
         for w in range(2):
@@ -214,14 +223,16 @@
 
 
 def layer_kernel(
-    neighbours, counts, ext, ext_bias, grad_out, w_query, w_key, w_value, w_out,
+    neighbours, counts, feat, key_bias, grad_out, w_query_hbm, w_key_hbm, w_value_hbm, w_out_hbm,
     out, grad_feat, grad_bias,
+    ext, near_bias, ext_bias, grad_rows, w_query, w_out, query, grad_att, key_value,
     part, halo, own, bias_sum, feat_parts, bias_parts, w_kv, gathered, scores, grad_probs, probs_low,
     scores_low, scores_rest, grad_kv, attended_t, grad_query_t, from_core, half, from_first, mine, from_second, total,
     core_send, core_recv, first_send, first_recv, second_send, second_recv,
     third_send, third_recv, fourth_send, fourth_recv,
     side, side_bias, rows_out, rows_bias, edge, edge_bias,
     side_send, side_recv, edge_send, edge_recv,
+    local_sem, wide_send, wide_recv, near_send, near_recv,
 ):
     lat = lax.axis_index("lat")
     lon = lax.axis_index("lon")
@@ -241,6 +252,10 @@
     base = core * NPEER
     other = (1 - core) * NPEER
 
+    off_lon = (lon + nlon - 1 + 2 * core) % nlon
+    off = (lat, off_lon)
+    seam = nlat // 2
+
     def plane_peer(index):
         x = index // 4
         return ((x // 2) * 4 + index % 4, (x % 2) * (2 * NZ) + z * 2 + core)
@@ -249,28 +264,128 @@
         return (lat, x_lo * (2 * NZ) + index * 2 + core)
 
     barrier = pltpu.get_barrier_semaphore()
+
     def greet(device):
         pl.semaphore_signal(barrier, inc=1, device_id=device, device_id_type=MESH)
 
-    greet(east)
-    greet(west)
-    pl.when(lat > 0)(lambda: greet(north))
-    pl.when(lat < nlat - 1)(lambda: greet(south))
+    greet(partner)
+    greet(off)
+
+    @pl.when(lat > 0)
+    def _():
+        greet((lat - 1, off_lon))
+        greet((lat - 1, partner[1]))
+
+    @pl.when(lat < nlat - 1)
+    def _():
+        greet((lat + 1, off_lon))
+        greet((lat + 1, partner[1]))
+
     @pl.loop(1, NXY)
     def _(step):
-        pl.semaphore_signal(barrier, inc=1, device_id=plane_peer((xy + step) % NXY), device_id_type=MESH)
+        greet(plane_peer((xy + step) % NXY))
 
     @pl.loop(1, NZ)
     def _(step):
-        pl.semaphore_signal(barrier, inc=1, device_id=depth_peer((z + step) % NZ), device_id_type=MESH)
+        greet(depth_peer((z + step) % NZ))
+
+    chans = feat.shape[3]
+    loads = [
+        (feat.at[0, 0], ext.at[4]),
+        (feat.at[0, 1], ext.at[7]),
+        (w_query_hbm, w_query),
+        (grad_out.at[0], grad_rows),
+        (w_out_hbm, w_out),
+        (w_key_hbm, w_kv.at[:, pl.ds(0, chans)]),
+        (w_value_hbm, w_kv.at[:, pl.ds(chans, chans)]),
+    ]
+    loads = [pltpu.make_async_copy(src, dst, local_sem.at[i]) for i, (src, dst) in enumerate(loads)]
+    for load in loads:
+        load.start()
+    near_bias[4] = key_bias[...]
+    loads[0].wait()
+    loads[1].wait()
+    inner = jnp.minimum(lat, 1) + jnp.minimum(nlat - 1 - lat, 1)
+    pl.semaphore_wait(barrier, NPEER + 2 * inner)
+
+    s_off = 4 + 3 * core
+    s_in = 7 - 3 * core
+    t_off = 9 - 9 * core
+    t_in = 9 * core
+    b_off = 2 - 2 * core
+    b_in = 2 * core
+
+    def wide_copy(source, target, order, device):
+        return remote(ext.at[source], ext.at[target], wide_send.at[order], wide_recv.at[target], device)
+
+    def near_copy(target, order, device):
+        return remote(near_bias.at[4], near_bias.at[target], near_send.at[order], near_recv.at[target], device)
+
+    def to_row(up):
+        device = north if up else south
+        corner = (lat - 1, off_lon) if up else (lat + 1, off_lon)
+        step, row, order = (1, 2, 0) if up else (-1, 0, 3)
+        wide_copy(s_in, s_in + step, order, device).start()
+        wide_copy(s_off, t_off + row, order + 1, corner).start()
+        wide_copy(s_off, s_off + step, order + 2, device).start()
+        near_copy(3 * row + 1, order, device).start()
+        near_copy(3 * row + b_off, order + 1, corner).start()
+        near_copy(3 * row + b_in, order + 2, (corner[0], partner[1])).start()
+
+    def wait_row(up):
+        step, row, order = (1, 2, 0) if up else (-1, 0, 3)
+        for k in range(3):
+            wide_copy(4, 4, order + k, partner).wait_send()
+            near_copy(4, order + k, partner).wait_send()
+
+    wide_copy(s_in, t_in + 1, 6, partner).start()
+    wide_copy(s_off, t_off + 1, 7, off).start()
+    near_copy(3 + b_in, 6, partner).start()
+    near_copy(3 + b_off, 7, off).start()
+    pl.when(lat == seam - 1)(lambda: to_row(False))
+    pl.when(lat > 0)(lambda: to_row(True))
+    pl.when((lat < nlat - 1) & (lat != seam - 1))(lambda: to_row(False))
+
+    for load in loads[2:]:
+        load.wait()
+    project(ext, grad_rows, w_query, w_out, w_kv, query, grad_att, key_value)
+
+    def pass_on(row, order):
+        slot = s_in - 1 + row
+        wide_copy(slot, slot, order, partner).wait_recv()
+        wide_copy(slot, t_in + row, order, partner).start()
+
+    pl.when(lat == seam - 1)(lambda: pass_on(0, 8))
+    pl.when(lat < nlat - 1)(lambda: pass_on(2, 9))
+    pl.when((lat > 0) & (lat != seam - 1))(lambda: pass_on(0, 8))
+
+    def arrived(row):
+        for slot in (s_off - 1 + row, t_in + row, t_off + row):
+            wide_copy(slot, slot, 0, partner).wait_recv()
+        for column in range(3):
+            near_copy(3 * row + column, 0, partner).wait_recv()
+
+    for slot in (t_in + 1, t_off + 1):
+        wide_copy(slot, slot, 0, partner).wait_recv()
+    for column in (0, 2):
+        near_copy(3 + column, 0, partner).wait_recv()
+    pl.when(lat > 0)(lambda: arrived(0))
+    pl.when(lat < nlat - 1)(lambda: arrived(2))
+    heads = ext_bias.shape[1]
+    for row in range(3):
+        west_bias = near_bias[3 * row].astype(F32)
+        own_bias = near_bias[3 * row + 1].astype(F32)
+        east_bias = near_bias[3 * row + 2].astype(F32)
+        ext_bias[row] = west_bias[heads:]
+        ext_bias[3 + row] = own_bias[:heads]
+        ext_bias[6 + row] = own_bias[heads:]
+        ext_bias[9 + row] = east_bias[:heads]
 
     all_picks, grad_query = attend(
-        neighbours, counts, ext, ext_bias, grad_out, w_query, w_key, w_value, w_out, part,
+        neighbours, counts, ext, ext_bias, grad_rows, query, grad_att, key_value, part,
         w_kv, gathered, scores, grad_probs, probs_low, scores_low, scores_rest, grad_kv,
         attended_t, grad_query_t, bias_parts,
     )
-    inner = jnp.minimum(lat, 1) + jnp.minimum(nlat - 1 - lat, 1)
-    pl.semaphore_wait(barrier, NPEER + inner)
 
     def side_copies(index):
         device = (west, east)[index]
@@ -305,10 +420,6 @@
         for chunk in chunks(step):
             core_copy(chunk).start()
 
-    scatter(all_picks, grad_query, w_query, w_kv, grad_kv, bias_parts, feat_parts, halo, own, bias_sum)
-    each(side_copies(0), "start")
-    each(side_copies(1), "start")
-
     @pl.loop(0, NZ)
     def _(step):
         a, b, c = chunks(step)
@@ -321,6 +432,10 @@
         def _():
             first_copy(b, plane_peer(b), xy).start()
             first_copy(c, depth_peer(c - NXY), NXY + z).start()
+
+    scatter(all_picks, grad_query, w_query, w_kv, grad_kv, bias_parts, feat_parts, halo, own, bias_sum)
+    each(side_copies(0), "start")
+    each(side_copies(1), "start")
 
     each(side_copies(0), "wait_recv")
     each(side_copies(1), "wait_recv")
@@ -465,14 +580,31 @@
         grad_feat[j] = total_grad.astype(BF)
         grad_bias[j] = bias_sum[3 * j + 4] + side_bias[j, 1] + (edge_bias[0, j] + edge_bias[1, j])
 
-
-def layer_call(neighbours, counts, ext, ext_bias, grad_out, w_query, w_key, w_value, w_out):
-    blocks, slots, chans = ext.shape
-    heads = ext_bias.shape[1]
+    wide_copy(4, 4, 6, partner).wait_send()
+    wide_copy(4, 4, 7, partner).wait_send()
+    near_copy(4, 6, partner).wait_send()
+    near_copy(4, 7, partner).wait_send()
+
+    @pl.when(lat > 0)
+    def _():
+        wait_row(True)
+        wide_copy(4, 4, 8, partner).wait_send()
+
+    @pl.when(lat < nlat - 1)
+    def _():
+        wait_row(False)
+        wide_copy(4, 4, 9, partner).wait_send()
+
+
+def layer_call(neighbours, counts, feat, key_bias, grad_out, w_query, w_key, w_value, w_out):
+    _, _, slots, chans = feat.shape
+    heads = key_bias.shape[0] // 2
+    blocks = 12
     entries = counts.shape[2]
     keys_all = entries * slots
     vmem = pl.BlockSpec(memory_space=pltpu.VMEM)
     smem = pl.BlockSpec(memory_space=pltpu.SMEM)
+    hbm = pl.BlockSpec(memory_space=pl.ANY)
     low = lambda *shape: pltpu.VMEM(shape, BF)
     wide = lambda *shape: pltpu.VMEM(shape, F32)
     dma = pltpu.SemaphoreType.DMA
@@ -483,9 +615,18 @@
             jax.ShapeDtypeStruct((2, slots, chans), BF),
             jax.ShapeDtypeStruct((2, heads, slots), F32),
         ],
-        in_specs=[smem] * 2 + [vmem] * 7,
+        in_specs=[smem] * 2 + [hbm, vmem] + [hbm] * 5,
         out_specs=[vmem] * 3,
         scratch_shapes=[
+            low(blocks, slots, chans),
+            low(9, 2 * heads, slots),
+            wide(blocks, heads, slots),
+            low(2, slots, chans),
+            low(chans, chans),
+            low(chans, chans),
+            low(2, slots, chans),
+            low(2, slots, chans),
+            low(2 * keys_all, 2 * chans),
             low(2 * NPEER, ROWS, chans),
             low(blocks, slots, chans),
             wide(2, slots, chans),
@@ -518,132 +659,11 @@
             low(2, 2, slots, chans),
             wide(2, 2, heads, slots),
         ]
-        + [dma((4,))] * 4,
+        + [dma((4,))] * 4
+        + [dma((7,)), dma((10,)), dma((12,)), dma((8,)), dma((9,))],
         compiler_params=pltpu.CompilerParams(collective_id=0, has_side_effects=True, vmem_limit_bytes=48 << 20),
         name="layer_backward",
-    )(neighbours, counts, ext, ext_bias, grad_out, w_query, w_key, w_value, w_out)
-
-
-def halo_kernel(feat, bias, ext, ext_bias, wide_send, wide_recv, bias_send, bias_recv):
-    lat = lax.axis_index("lat")
-    lon = lax.axis_index("lon")
-    nlat = lax.axis_size("lat")
-    nlon = lax.axis_size("lon")
-    core = lon % 2
-    east = (lat, (lon + 1) % nlon)
-    west = (lat, (lon + nlon - 1) % nlon)
-    north = (lat - 1, lon)
-    south = (lat + 1, lon)
-    barrier = pltpu.get_barrier_semaphore()
-
-    def greet(device):
-        pl.semaphore_signal(barrier, inc=1, device_id=device, device_id_type=MESH)
-
-    greet(east)
-    greet(west)
-    pl.when(lat > 0)(lambda: greet(north))
-    pl.when(lat < nlat - 1)(lambda: greet(south))
-    for j in range(2):
-        ext[3 * j + 4] = feat[j]
-        ext_bias[3 * j + 4] = bias[j].astype(F32)
-    inner = jnp.minimum(lat, 1) + jnp.minimum(nlat - 1 - lat, 1)
-    pl.semaphore_wait(barrier, 2 + inner)
-
-    def copies(source, target, order, device):
-        return (
-            remote(ext.at[source], ext.at[target], wide_send.at[order], wide_recv.at[target], device),
-            remote(ext_bias.at[source], ext_bias.at[target], bias_send.at[order], bias_recv.at[target], device),
-        )
-
-    def start(*args):
-        for copy in copies(*args):
-            copy.start()
-
-    def wait_recv(slot):
-        for copy in copies(slot, slot, 0, east):
-            copy.wait_recv()
-
-    def wait_send(order):
-        for copy in copies(4, 4, order, east):
-            copy.wait_send()
-
-    first = 4 + 3 * core
-    second = 7 - 3 * core
-
-    def to_north():
-        start(first, first + 1, 0, north)
-        start(second, second + 1, 1, north)
-
-    def to_south():
-        start(first, first - 1, 2, south)
-        start(second, second - 1, 3, south)
-
-    seam = nlat // 2
-    pl.when(lat == seam - 1)(to_south)
-    pl.when(lat > 0)(to_north)
-    pl.when((lat < nlat - 1) & (lat != seam - 1))(to_south)
-    start(7, 1, 4, east)
-    start(4, 10, 5, west)
-
-    def pass_on(row, order):
-        def send_west():
-            wait_recv(3 + row)
-            start(3 + row, 9 + row, order, west)
-
-        def send_east():
-            wait_recv(6 + row)
-            start(6 + row, row, order + 1, east)
-
-        @pl.when(core == 0)
-        def _():
-            send_west()
-            send_east()
-
-        @pl.when(core == 1)
-        def _():
-            send_east()
-            send_west()
-
-    pl.when(lat == seam - 1)(lambda: pass_on(0, 8))
-    pl.when(lat < nlat - 1)(lambda: pass_on(2, 6))
-    pl.when((lat > 0) & (lat != seam - 1))(lambda: pass_on(0, 8))
-    wait_recv(1)
-    wait_recv(10)
-    wait_send(4)
-    wait_send(5)
-
-    @pl.when(lat > 0)
-    def _():
-        wait_recv(0)
-        wait_recv(9)
-        for order in (0, 1, 8, 9):
-            wait_send(order)
-
-    @pl.when(lat < nlat - 1)
-    def _():
-        wait_recv(2)
-        wait_recv(11)
-        for order in (2, 3, 6, 7):
-            wait_send(order)
-
-
-def halo_call(feat, bias):
-    _, slots, chans = feat.shape
-    heads = bias.shape[1]
-    vmem = pl.BlockSpec(memory_space=pltpu.VMEM)
-    dma = pltpu.SemaphoreType.DMA
-    return pl.pallas_call(
-        halo_kernel,
-        out_shape=[
-            jax.ShapeDtypeStruct((12, slots, chans), BF),
-            jax.ShapeDtypeStruct((12, heads, slots), F32),
-        ],
-        in_specs=[vmem] * 2,
-        out_specs=[vmem] * 2,
-        scratch_shapes=[dma((10,)), dma((12,)), dma((10,)), dma((12,))],
-        compiler_params=pltpu.CompilerParams(collective_id=1, has_side_effects=True, vmem_limit_bytes=16 << 20),
-        name="gather_halo",
-    )(feat, bias)
+    )(neighbours, counts, feat, key_bias, grad_out, w_query, w_key, w_value, w_out)
 
 
 def per_device(
@@ -651,9 +671,9 @@
 ):
     brows, bcols, slots, chans = features.shape
     heads = key_bias.shape[2]
-    ext, ext_bias = halo_call(features[0], key_bias[0])
     low, grad_features, grad_bias = layer_call(
-        neighbours, key_counts, ext, ext_bias, grad_out[0], w_query, w_key, w_value, w_out
+        neighbours, key_counts, features, key_bias.reshape(bcols * heads, slots), grad_out,
+        w_query, w_key, w_value, w_out,
     )
     cells = lax.axis_size("lat") * lax.axis_size("lon") * brows * bcols * slots
     summed = low.astype(F32).reshape(4, chans, chans) * float(cells) ** (-0.5)

time: 76 us -> 77.9 us (1.025)
  Pallas kernels: 64.2 us -> 66.2 us
    pallas_call x1, Pallas kernels: 50 us -> 66.2 us  [layer_call(): pl.pallas_call(layer_kernel, out_shape=[jax.ShapeDtypeStruct((2 * NPEER,...]
    pallas_call x1 -> x0, Pallas kernels: 14.2 us -> none  [halo_call(): pl.pallas_call(halo_kernel, out_shape=[jax.ShapeDtypeStruct((12, slots, c...]
where the time goes in v2:
time: 77.9 us; the launch traced here: 77.6 us
  Pallas kernels  66.2 us (85%)
  local copies, waits for them, and re-layouts  10.5 us (13%)
    pallas_call x1, Pallas kernels, layer_call(): pl.pallas_call(layer_kernel, out_shape=[jax.ShapeDtypeStruct((2 * NPEER,...  66.2 us
    unnamed x20, local copies, waits for them, and re-layouts  9.01 us

profile of v2, /device:TPU:1, one launch (start us, length us, event | category | flops | bytes accessed | tf_op | source)
XLA Modules:
  0.0 77.6 jit_solution(7873617250855242416)
XLA Ops:
  0.6 0.0 copy-start
  0.6 1.0 %copy-done = bf16[384,384]{1,0:T(8,128)(2,1)S(1)} copy-done((bf16[384,384]{1,0:T(8,128)(2,1)S(1)}, bf16[384,384]{1,0:T(8,128)(2,1)}, u32[]{:S(2)}) %copy-start) | copy-done | bytes 294936
  1.6 0.0 copy-start.1
  1.6 1.0 %copy-done.1 = bf16[384,384]{1,0:T(8,128)(2,1)S(1)} copy-done((bf16[384,384]{1,0:T(8,128)(2,1)S(1)}, bf16[384,384]{1,0:T(8,128)(2,1)}, u32[]{:S(2)}) %copy-start.1) | copy-done | bytes 294936
  2.6 0.0 copy-start.2
  2.6 1.0 %copy-done.2 = bf16[384,384]{1,0:T(8,128)(2,1)S(1)} copy-done((bf16[384,384]{1,0:T(8,128)(2,1)S(1)}, bf16[384,384]{1,0:T(8,128)(2,1)}, u32[]{:S(2)}) %copy-start.2) | copy-done | bytes 294936
  3.5 0.0 copy-start.3
  3.5 1.0 %copy-done.3 = bf16[384,384]{1,0:T(8,128)(2,1)S(1)} copy-done((bf16[384,384]{1,0:T(8,128)(2,1)S(1)}, bf16[384,384]{1,0:T(8,128)(2,1)}, u32[]{:S(2)}) %copy-start.3) | copy-done | bytes 294936
  4.5 0.0 copy-start.4
  4.5 0.9 %copy-done.4 = bf16[1,2,128,384]{3,2,1,0:T(8,128)(2,1)S(1)} copy-done((bf16[1,2,128,384]{3,2,1,0:T(8,128)(2,1)S(1)}, bf16[1,2,128,384]{3,2,1,0:T(8,128)(2,1)}, u32[]{:S(2)}) %copy-start.4) | copy-done | bytes 196632
  5.4 0.0 copy-start.5
  5.4 0.9 %copy-done.5 = bf16[1,2,128,384]{3,2,1,0:T(8,128)(2,1)S(1)} copy-done((bf16[1,2,128,384]{3,2,1,0:T(8,128)(2,1)S(1)}, bf16[1,2,128,384]{3,2,1,0:T(8,128)(2,1)}, u32[]{:S(2)}) %copy-start.5) | copy-done | bytes 196632
  6.3 0.0 copy-start.6
  6.3 0.7 copy-done.6
  7.0 0.0 copy-start.7
  7.0 0.7 copy-done.7
  7.7 0.0 copy-start.8
  7.7 0.7 copy-done.8
  8.4 66.2 %layer_backward.1 = (bf16[48,32,384]{2,1,0:T(8,128)(2,1)S(1)}, bf16[2,128,384]{2,1,0:T(8,128)(2,1)S(1)}, f32[2,8,128]{2,1,0:T(8,128)S(1)}) custom-call(s32[1,2,4]{2,1,0:T(2,128)S(1)} %copy-done.7, s32[1,2,4]{2,1,0:T(2,128)S(1)} %copy-done.8, bf16[1,2,128,384]{3,2,1,0:T(8,128)(2,1)S(1)} %copy-done.4, bf16[16,128]{1,0:T(8,128)(2,1)S(1)} %bitcast.9, ...), custom_call_target="tpu_custom_call" | custom-call | tf_op jit(solution)/shard_map/layer_backward/pallas_call | solution.py:611
  74.6 0.3 convert_multiply_fusion
  74.9 1.4 %fusion = (f32[12,32,384]{2,1,0:T(8,128)}, f32[12,32,384]{2,1,0:T(8,128)}, f32[12,32,384]{2,1,0:T(8,128)}, f32[12,32,384]{2,1,0:T(8,128)}) fusion(f32[48,32,384]{2,1,0:T(8,128)S(1)} %convert_multiply_fusion), kind=kLoop, calls=%fused_computation.1 | loop fusion | bytes 4718592 | tf_op jit(solution)/shard_map/slice | solution.py:686
  76.3 0.7 copy.17
  77.0 0.6 copy.18
Async XLA Ops:
  0.6 1.0 %copy-start = (bf16[384,384]{1,0:T(8,128)(2,1)S(1)}, bf16[384,384]{1,0:T(8,128)(2,1)}, u32[]{:S(2)}) copy-start(bf16[384,384]{1,0:T(8,128)(2,1)} %w_query_hbm.1) | copy-start | bytes 884740
  1.6 1.0 %copy-start.1 = (bf16[384,384]{1,0:T(8,128)(2,1)S(1)}, bf16[384,384]{1,0:T(8,128)(2,1)}, u32[]{:S(2)}) copy-start(bf16[384,384]{1,0:T(8,128)(2,1)} %w_key_hbm.1) | copy-start | bytes 884740
  2.6 1.0 %copy-start.2 = (bf16[384,384]{1,0:T(8,128)(2,1)S(1)}, bf16[384,384]{1,0:T(8,128)(2,1)}, u32[]{:S(2)}) copy-start(bf16[384,384]{1,0:T(8,128)(2,1)} %w_value_hbm.1) | copy-start | bytes 884740
  3.5 1.0 %copy-start.3 = (bf16[384,384]{1,0:T(8,128)(2,1)S(1)}, bf16[384,384]{1,0:T(8,128)(2,1)}, u32[]{:S(2)}) copy-start(bf16[384,384]{1,0:T(8,128)(2,1)} %w_out_hbm.1) | copy-start | bytes 884740
  4.5 0.9 %copy-start.4 = (bf16[1,2,128,384]{3,2,1,0:T(8,128)(2,1)S(1)}, bf16[1,2,128,384]{3,2,1,0:T(8,128)(2,1)}, u32[]{:S(2)}) copy-start(bf16[1,2,128,384]{3,2,1,0:T(8,128)(2,1)} %feat.1) | copy-start | bytes 589828
  5.4 0.9 %copy-start.5 = (bf16[1,2,128,384]{3,2,1,0:T(8,128)(2,1)S(1)}, bf16[1,2,128,384]{3,2,1,0:T(8,128)(2,1)}, u32[]{:S(2)}) copy-start(bf16[1,2,128,384]{3,2,1,0:T(8,128)(2,1)} %grad_out.1) | copy-start | bytes 589828
  6.3 0.7 copy-start.6
  7.0 0.7 copy-start.7
  7.7 0.7 copy-start.8

commit v3 on v2

--- a/solution.py
+++ b/solution.py
@@ -1,3 +1,4 @@
+import functools
 import math
 
 import jax
@@ -223,16 +224,16 @@
 
 
 def layer_kernel(
-    neighbours, counts, feat, key_bias, grad_out, w_query_hbm, w_key_hbm, w_value_hbm, w_out_hbm,
+    neighbours_hbm, counts_hbm, feat, key_bias, grad_out, w_query_hbm, w_key_hbm, w_value_hbm, w_out_hbm,
     out, grad_feat, grad_bias,
-    ext, near_bias, ext_bias, grad_rows, w_query, w_out, query, grad_att, key_value,
+    neighbours, counts, ext, near_bias, ext_bias, grad_rows, w_query, w_out, query, grad_att, key_value,
     part, halo, own, bias_sum, feat_parts, bias_parts, w_kv, gathered, scores, grad_probs, probs_low,
-    scores_low, scores_rest, grad_kv, attended_t, grad_query_t, from_core, half, from_first, mine, from_second, total,
+    scores_low, scores_rest, grad_kv, attended_t, grad_query_t,
+    from_core, half, from_first, mine, from_second, total, summed,
+    side, side_bias, rows_out, rows_bias, edge, edge_bias,
+    local_sem, out_sem, wide_send, wide_recv, near_send, near_recv,
     core_send, core_recv, first_send, first_recv, second_send, second_recv,
-    third_send, third_recv, fourth_send, fourth_recv,
-    side, side_bias, rows_out, rows_bias, edge, edge_bias,
-    side_send, side_recv, edge_send, edge_recv,
-    local_sem, wide_send, wide_recv, near_send, near_recv,
+    third_send, third_recv, fourth_send, fourth_recv, side_send, side_recv, edge_send, edge_recv,
 ):
     lat = lax.axis_index("lat")
     lon = lax.axis_index("lon")
@@ -268,6 +269,23 @@
     def greet(device):
         pl.semaphore_signal(barrier, inc=1, device_id=device, device_id_type=MESH)
 
+    def settle(like, sem):
+        pltpu.make_async_copy(like, like, sem).wait()
+
+    chans = feat.shape[3]
+    loads = [
+        (feat.at[0, 0], ext.at[4], 0),
+        (feat.at[0, 1], ext.at[7], 0),
+        (w_query_hbm, w_query, 1),
+        (grad_out.at[0], grad_rows, 2),
+        (w_out_hbm, w_out, 3),
+        (w_key_hbm, w_kv.at[:, pl.ds(0, chans)], 4),
+        (w_value_hbm, w_kv.at[:, pl.ds(chans, chans)], 4),
+        (neighbours_hbm, neighbours, 5),
+        (counts_hbm, counts, 6),
+    ]
+    for src, dst, index in loads:
+        pltpu.make_async_copy(src, dst, local_sem.at[index]).start()
     greet(partner)
     greet(off)
 
@@ -289,22 +307,8 @@
     def _(step):
         greet(depth_peer((z + step) % NZ))
 
-    chans = feat.shape[3]
-    loads = [
-        (feat.at[0, 0], ext.at[4]),
-        (feat.at[0, 1], ext.at[7]),
-        (w_query_hbm, w_query),
-        (grad_out.at[0], grad_rows),
-        (w_out_hbm, w_out),
-        (w_key_hbm, w_kv.at[:, pl.ds(0, chans)]),
-        (w_value_hbm, w_kv.at[:, pl.ds(chans, chans)]),
-    ]
-    loads = [pltpu.make_async_copy(src, dst, local_sem.at[i]) for i, (src, dst) in enumerate(loads)]
-    for load in loads:
-        load.start()
     near_bias[4] = key_bias[...]
-    loads[0].wait()
-    loads[1].wait()
+    settle(ext.at[pl.ds(0, 2)], local_sem.at[0])
     inner = jnp.minimum(lat, 1) + jnp.minimum(nlat - 1 - lat, 1)
     pl.semaphore_wait(barrier, NPEER + 2 * inner)
 
@@ -315,60 +319,56 @@
     b_off = 2 - 2 * core
     b_in = 2 * core
 
-    def wide_copy(source, target, order, device):
-        return remote(ext.at[source], ext.at[target], wide_send.at[order], wide_recv.at[target], device)
-
-    def near_copy(target, order, device):
-        return remote(near_bias.at[4], near_bias.at[target], near_send.at[order], near_recv.at[target], device)
+    def wide_copy(source, target, sent, landed, device):
+        return remote(ext.at[source], ext.at[target], wide_send.at[sent], wide_recv.at[landed], device)
+
+    def near_copy(target, sent, landed, device):
+        return remote(near_bias.at[4], near_bias.at[target], near_send.at[sent], near_recv.at[landed], device)
 
     def to_row(up):
         device = north if up else south
         corner = (lat - 1, off_lon) if up else (lat + 1, off_lon)
-        step, row, order = (1, 2, 0) if up else (-1, 0, 3)
-        wide_copy(s_in, s_in + step, order, device).start()
-        wide_copy(s_off, t_off + row, order + 1, corner).start()
-        wide_copy(s_off, s_off + step, order + 2, device).start()
-        near_copy(3 * row + 1, order, device).start()
-        near_copy(3 * row + b_off, order + 1, corner).start()
-        near_copy(3 * row + b_in, order + 2, (corner[0], partner[1])).start()
-
-    def wait_row(up):
-        step, row, order = (1, 2, 0) if up else (-1, 0, 3)
-        for k in range(3):
-            wide_copy(4, 4, order + k, partner).wait_send()
-            near_copy(4, order + k, partner).wait_send()
-
-    wide_copy(s_in, t_in + 1, 6, partner).start()
-    wide_copy(s_off, t_off + 1, 7, off).start()
-    near_copy(3 + b_in, 6, partner).start()
-    near_copy(3 + b_off, 7, off).start()
+        inside = (corner[0], partner[1])
+        step, row, sent, landed = (1, 2, 1, 2) if up else (-1, 0, 2, 1)
+        wide_copy(s_in, s_in + step, sent, landed, device).start()
+        wide_copy(s_off, t_off + row, sent, landed + 2, corner).start()
+        wide_copy(s_off, s_off + step, sent, landed + 2, device).start()
+        near_copy(3 * row + 1, sent, landed, device).start()
+        near_copy(3 * row + b_off, sent, landed, corner).start()
+        near_copy(3 * row + b_in, sent, landed, inside).start()
+
+    wide_copy(s_in, t_in + 1, 0, 0, partner).start()
+    wide_copy(s_off, t_off + 1, 0, 0, off).start()
+    near_copy(3 + b_in, 0, 0, partner).start()
+    near_copy(3 + b_off, 0, 0, off).start()
     pl.when(lat == seam - 1)(lambda: to_row(False))
     pl.when(lat > 0)(lambda: to_row(True))
     pl.when((lat < nlat - 1) & (lat != seam - 1))(lambda: to_row(False))
 
-    for load in loads[2:]:
-        load.wait()
+    settle(w_query, local_sem.at[1])
+    settle(grad_rows, local_sem.at[2])
+    settle(w_out, local_sem.at[3])
+    settle(w_kv, local_sem.at[4])
+    settle(neighbours, local_sem.at[5])
+    settle(counts, local_sem.at[6])
     project(ext, grad_rows, w_query, w_out, w_kv, query, grad_att, key_value)
 
-    def pass_on(row, order):
+    def pass_on(row):
+        landed = 1 + row // 2
         slot = s_in - 1 + row
-        wide_copy(slot, slot, order, partner).wait_recv()
-        wide_copy(slot, t_in + row, order, partner).start()
-
-    pl.when(lat == seam - 1)(lambda: pass_on(0, 8))
-    pl.when(lat < nlat - 1)(lambda: pass_on(2, 9))
-    pl.when((lat > 0) & (lat != seam - 1))(lambda: pass_on(0, 8))
+        settle(ext.at[slot], wide_recv.at[landed])
+        wide_copy(slot, t_in + row, landed + 2, landed + 2, partner).start()
 
     def arrived(row):
-        for slot in (s_off - 1 + row, t_in + row, t_off + row):
-            wide_copy(slot, slot, 0, partner).wait_recv()
-        for column in range(3):
-            near_copy(3 * row + column, 0, partner).wait_recv()
-
-    for slot in (t_in + 1, t_off + 1):
-        wide_copy(slot, slot, 0, partner).wait_recv()
-    for column in (0, 2):
-        near_copy(3 + column, 0, partner).wait_recv()
+        landed = 1 + row // 2
+        settle(ext.at[pl.ds(0, 3)], wide_recv.at[landed + 2])
+        settle(near_bias.at[pl.ds(0, 3)], near_recv.at[landed])
+
+    pl.when(lat == seam - 1)(lambda: pass_on(0))
+    pl.when(lat < nlat - 1)(lambda: pass_on(2))
+    pl.when((lat > 0) & (lat != seam - 1))(lambda: pass_on(0))
+    settle(ext.at[pl.ds(0, 2)], wide_recv.at[0])
+    settle(near_bias.at[pl.ds(0, 2)], near_recv.at[0])
     pl.when(lat > 0)(lambda: arrived(0))
     pl.when(lat < nlat - 1)(lambda: arrived(2))
     heads = ext_bias.shape[1]
@@ -387,173 +387,117 @@
         attended_t, grad_query_t, bias_parts,
     )
 
-    def side_copies(index):
+    plane = pl.ds(0, NXY)
+    depth = pl.ds(NXY, NZ)
+
+    def core_copy(which):
+        start, count = ((0, NXY), (NXY, NZ))[which]
+        return remote(
+            part.at[pl.ds(other + start, count)], from_core.at[pl.ds(start, count)],
+            core_send.at[which], core_recv.at[which], partner,
+        )
+
+    core_copy(1).start()
+    core_copy(0).start()
+
+    def add_core(start, count):
+        mine_rows = part[pl.ds(base + start, count)].astype(F32)
+        half[pl.ds(start, count)] = (mine_rows + from_core[pl.ds(start, count)].astype(F32)).astype(BF)
+
+    core_copy(1).wait_recv()
+    add_core(NXY, NZ)
+
+    @pl.loop(1, NZ)
+    def _(step):
+        peer = (z + step) % NZ
+        remote(half.at[NXY + peer], from_first.at[NXY + z], first_send.at[1], first_recv.at[1], depth_peer(peer)).start()
+
+    core_copy(0).wait_recv()
+    add_core(0, NXY)
+
+    @pl.loop(1, NXY)
+    def _(step):
+        peer = (xy + step) % NXY
+        remote(half.at[peer], from_first.at[xy], first_send.at[0], first_recv.at[0], plane_peer(peer)).start()
+
+    from_first[xy] = half[xy]
+    from_first[NXY + z] = half[NXY + z]
+    scatter(all_picks, grad_query, w_query, w_kv, grad_kv, bias_parts, feat_parts, halo, own, bias_sum)
+    for index in range(2):
         device = (west, east)[index]
-        source = pl.ds(9 * index, 3)
-        return (
-            remote(halo.at[source], side.at[1 - index], side_send.at[2 * index], side_recv.at[2 - 2 * index], device),
-            remote(bias_sum.at[source], side_bias.at[1 - index], side_send.at[2 * index + 1], side_recv.at[3 - 2 * index], device),
-        )
-
-    def edge_copies(index):
-        device = (north, south)[index]
-        return (
-            remote(rows_out.at[index], edge.at[1 - index], edge_send.at[2 * index], edge_recv.at[2 - 2 * index], device),
-            remote(rows_bias.at[index], edge_bias.at[1 - index], edge_send.at[2 * index + 1], edge_recv.at[3 - 2 * index], device),
-        )
-
-    def each(copies, what):
-        for copy in copies:
-            getattr(copy, what)()
-
-    def chunks(step):
-        return ((xy + 2 * step + 1) % NXY, (xy + 2 * step + 2) % NXY, NXY + (z + step + 1) % NZ)
-
-    def core_copy(chunk):
-        return remote(part.at[other + chunk], from_core.at[chunk], core_send.at[chunk], core_recv.at[chunk], partner)
-
-    def first_copy(chunk, device, slot):
-        return remote(half.at[chunk], from_first.at[slot], first_send.at[chunk], first_recv.at[slot], device)
-
-    @pl.loop(0, NZ)
+        columns = pl.ds(9 * index, 3)
+        remote(halo.at[columns], side.at[1 - index], side_send.at[0], side_recv.at[0], device).start()
+        remote(bias_sum.at[columns], side_bias.at[1 - index], side_send.at[1], side_recv.at[1], device).start()
+
+    settle(half.at[pl.ds(0, NZ - 1)], first_recv.at[1])
+    mine[1] = jnp.sum(from_first[depth].astype(F32), axis=0).astype(BF)
+
+    @pl.loop(1, NXY)
     def _(step):
-        for chunk in chunks(step):
-            core_copy(chunk).start()
-
-    @pl.loop(0, NZ)
+        peer = (xy + step) % NXY
+        remote(mine.at[1], from_second.at[xy], second_send.at[1], second_recv.at[1], plane_peer(peer)).start()
+
+    settle(half.at[pl.ds(0, NXY - 1)], first_recv.at[0])
+    mine[0] = jnp.sum(from_first[plane].astype(F32), axis=0).astype(BF)
+
+    @pl.loop(1, NZ)
     def _(step):
-        a, b, c = chunks(step)
-        for chunk in (a, b, c):
-            core_copy(chunk).wait_recv()
-            half[chunk] = (part[base + chunk].astype(jnp.float32) + from_core[chunk].astype(jnp.float32)).astype(jnp.bfloat16)
-        first_copy(a, plane_peer(a), xy).start()
-
-        @pl.when(step < NZ - 1)
-        def _():
-            first_copy(b, plane_peer(b), xy).start()
-            first_copy(c, depth_peer(c - NXY), NXY + z).start()
-
-    scatter(all_picks, grad_query, w_query, w_kv, grad_kv, bias_parts, feat_parts, halo, own, bias_sum)
-    each(side_copies(0), "start")
-    each(side_copies(1), "start")
-
-    each(side_copies(0), "wait_recv")
-    each(side_copies(1), "wait_recv")
+        peer = (z + step) % NZ
+        remote(mine.at[0], from_second.at[NXY + z], second_send.at[0], second_recv.at[0], depth_peer(peer)).start()
+
+    from_second[xy] = mine[1]
+    from_second[NXY + z] = mine[0]
+
+    settle(side, side_recv.at[0])
+    settle(side_bias, side_recv.at[1])
     for index in range(2):
         for j in range(2):
             slot = 3 * j + 3 + 2 * index
             rows_out[index, j] = (halo[slot].astype(F32) + side[j, 2 * index].astype(F32)).astype(BF)
             rows_bias[index, j] = bias_sum[slot] + side_bias[j, 2 * index]
-    pl.when(lat > 0)(lambda: each(edge_copies(0), "start"))
-    pl.when(lat < nlat - 1)(lambda: each(edge_copies(1), "start"))
-
-    from_first[xy] = half[xy]
-    from_first[NXY + z] = half[NXY + z]
-
-    def wait_first(step, index):
-        slot = index
-        first_copy(slot, partner, slot).wait_recv()
+
+    def to_edge(index):
+        device = (north, south)[index]
+        landed = 2 - 2 * index
+        remote(rows_out.at[index], edge.at[1 - index], edge_send.at[2 * index], edge_recv.at[landed], device).start()
+        remote(rows_bias.at[index], edge_bias.at[1 - index], edge_send.at[2 * index + 1], edge_recv.at[landed + 1], device).start()
+
+    pl.when(lat == seam - 1)(lambda: to_edge(1))
+    pl.when(lat > 0)(lambda: to_edge(0))
+    pl.when((lat < nlat - 1) & (lat != seam - 1))(lambda: to_edge(1))
+
+    settle(half.at[pl.ds(0, NXY - 1)], second_recv.at[1])
+    total[1] = jnp.sum(from_second[plane].astype(F32), axis=0).astype(BF)
 
     @pl.loop(1, NZ)
     def _(step):
-        wait_first(step, NXY + (z - step + NZ) % NZ)
-
-    mine[1] = jnp.sum(from_first[NXY:NPEER].astype(jnp.float32), axis=0).astype(jnp.bfloat16)
-
-    def second_b(index):
-        return remote(mine.at[1], from_second.at[xy], second_send.at[index], second_recv.at[xy], plane_peer(index))
-
-    def second_a(index):
-        return remote(mine.at[0], from_second.at[NXY + z], second_send.at[NXY + index], second_recv.at[NXY + z], depth_peer(index))
+        peer = (z + step) % NZ
+        remote(total.at[1], summed.at[base + NXY + z], third_send.at[1], third_recv.at[1], depth_peer(peer)).start()
+
+    summed[base + NXY + z] = total[1]
+    settle(half.at[pl.ds(0, NZ - 1)], second_recv.at[0])
+    total[0] = jnp.sum(from_second[depth].astype(F32), axis=0).astype(BF)
 
     @pl.loop(1, NXY)
     def _(step):
-        second_b((xy + step) % NXY).start()
-
-    @pl.loop(1, NXY)
-    def _(step):
-        wait_first(step, (xy - step + NXY) % NXY)
-
-    mine[0] = jnp.sum(from_first[0:NXY].astype(jnp.float32), axis=0).astype(jnp.bfloat16)
-
-    @pl.loop(1, NZ)
-    def _(step):
-        second_a((z + step) % NZ).start()
-
-    from_second[xy] = mine[1]
-    from_second[NXY + z] = mine[0]
-
-    def wait_second(slot):
-        remote(mine.at[0], from_second.at[slot], second_send.at[slot], second_recv.at[slot], partner).wait_recv()
-
-    def third_copy(which, slot, index, device):
-        return remote(total.at[which], out.at[slot], third_send.at[index], third_recv.at[slot], device)
-
-    def fourth_copy(slot):
-        return remote(out.at[slot], out.at[slot], fourth_send.at[slot], fourth_recv.at[slot], partner)
-
-    @pl.loop(1, NXY)
-    def _(step):
-        wait_second((xy - step + NXY) % NXY)
-
-    total[1] = jnp.sum(from_second[0:NXY].astype(jnp.float32), axis=0).astype(jnp.bfloat16)
-
-    @pl.loop(1, NZ)
-    def _(step):
-        index = (z + step) % NZ
-        third_copy(1, base + NXY + z, NXY + index, depth_peer(index)).start()
-
-    out[base + NXY + z] = total[1]
-    fourth_copy(base + NXY + z).start()
-
-    @pl.loop(1, NZ)
-    def _(step):
-        wait_second(NXY + (z - step + NZ) % NZ)
-
-    total[0] = jnp.sum(from_second[NXY:NPEER].astype(jnp.float32), axis=0).astype(jnp.bfloat16)
-
-    @pl.loop(1, NXY)
-    def _(step):
-        index = (xy + step) % NXY
-        third_copy(0, base + xy, index, plane_peer(index)).start()
-
-    out[base + xy] = total[0]
-    fourth_copy(base + xy).start()
-
-    def forward(slot):
-        third_copy(0, slot, 0, partner).wait_recv()
-        fourth_copy(slot).start()
-
-    @pl.loop(1, NZ)
-    def _(step):
-        forward(base + NXY + (z - step + NZ) % NZ)
-
-    @pl.loop(1, NXY)
-    def _(step):
-        forward(base + (xy - step + NXY) % NXY)
-
-    @pl.loop(0, NPEER)
-    def _(chunk):
-        core_copy(chunk).wait_send()
-        fourth_copy(base + chunk).wait_send()
-        fourth_copy(other + chunk).wait_recv()
-
-    @pl.loop(1, NXY)
-    def _(step):
-        index = (xy + step) % NXY
-        first_copy(index, partner, index).wait_send()
-        second_b(index).wait_send()
-        third_copy(0, base + xy, index, partner).wait_send()
-
-    @pl.loop(1, NZ)
-    def _(step):
-        index = (z + step) % NZ
-        first_copy(NXY + index, partner, index).wait_send()
-        second_a(index).wait_send()
-        third_copy(1, base + xy, NXY + index, partner).wait_send()
-
-    each(side_copies(0), "wait_send")
-    each(side_copies(1), "wait_send")
+        peer = (xy + step) % NXY
+        remote(total.at[0], summed.at[base + xy], third_send.at[0], third_recv.at[0], plane_peer(peer)).start()
+
+    summed[base + xy] = total[0]
+
+    def fourth_copy(which):
+        start, count = ((0, NXY), (NXY, NZ))[which]
+        rows = summed.at[pl.ds(base + start, count)]
+        return remote(rows, rows, fourth_send.at[0], fourth_recv.at[0], partner)
+
+    settle(half.at[pl.ds(0, NZ - 1)], third_recv.at[1])
+    fourth_copy(1).start()
+    settle(half.at[pl.ds(0, NXY - 1)], third_recv.at[0])
+    fourth_copy(0).start()
+    own_rows = pl.ds(base, NPEER)
+    other_rows = pl.ds(other, NPEER)
+    own_out = pltpu.make_async_copy(summed.at[own_rows], out.at[own_rows], out_sem.at[0])
+    own_out.start()
 
     @pl.when(lat == 0)
     def _():
@@ -567,33 +511,51 @@
 
     @pl.when(lat > 0)
     def _():
-        each(edge_copies(0), "wait_send")
-        each(edge_copies(1), "wait_recv")
+        settle(rows_out.at[0], edge_send.at[0])
+        settle(rows_bias.at[0], edge_send.at[1])
+        settle(edge.at[0], edge_recv.at[0])
+        settle(edge_bias.at[0], edge_recv.at[1])
 
     @pl.when(lat < nlat - 1)
     def _():
-        each(edge_copies(1), "wait_send")
-        each(edge_copies(0), "wait_recv")
+        settle(rows_out.at[1], edge_send.at[2])
+        settle(rows_bias.at[1], edge_send.at[3])
+        settle(edge.at[1], edge_recv.at[2])
+        settle(edge_bias.at[1], edge_recv.at[3])
 
     for j in range(2):
         total_grad = own[j] + side[j, 1].astype(F32) + (edge[0, j].astype(F32) + edge[1, j].astype(F32))
         grad_feat[j] = total_grad.astype(BF)
         grad_bias[j] = bias_sum[3 * j + 4] + side_bias[j, 1] + (edge_bias[0, j] + edge_bias[1, j])
 
-    wide_copy(4, 4, 6, partner).wait_send()
-    wide_copy(4, 4, 7, partner).wait_send()
-    near_copy(4, 6, partner).wait_send()
-    near_copy(4, 7, partner).wait_send()
+    settle(ext.at[pl.ds(0, 2)], wide_send.at[0])
+    settle(near_bias.at[pl.ds(0, 2)], near_send.at[0])
 
     @pl.when(lat > 0)
     def _():
-        wait_row(True)
-        wide_copy(4, 4, 8, partner).wait_send()
+        settle(ext.at[pl.ds(0, 3)], wide_send.at[1])
+        settle(ext.at[0], wide_send.at[3])
+        settle(near_bias.at[pl.ds(0, 3)], near_send.at[1])
 
     @pl.when(lat < nlat - 1)
     def _():
-        wait_row(False)
-        wide_copy(4, 4, 9, partner).wait_send()
+        settle(ext.at[pl.ds(0, 3)], wide_send.at[2])
+        settle(ext.at[0], wide_send.at[4])
+        settle(near_bias.at[pl.ds(0, 3)], near_send.at[2])
+
+    core_copy(0).wait_send()
+    core_copy(1).wait_send()
+    settle(side, side_send.at[0])
+    settle(side_bias, side_send.at[1])
+    for sems, wide_index in ((first_send, 0), (second_send, 1), (third_send, 0)):
+        settle(half.at[pl.ds(0, NXY - 1)], sems.at[wide_index])
+        settle(half.at[pl.ds(0, NZ - 1)], sems.at[1 - wide_index])
+    settle(half, fourth_send.at[0])
+    settle(half, fourth_recv.at[0])
+    other_out = pltpu.make_async_copy(summed.at[other_rows], out.at[other_rows], out_sem.at[1])
+    other_out.start()
+    own_out.wait()
+    other_out.wait()
 
 
 def layer_call(neighbours, counts, feat, key_bias, grad_out, w_query, w_key, w_value, w_out):
@@ -603,7 +565,6 @@
     entries = counts.shape[2]
     keys_all = entries * slots
     vmem = pl.BlockSpec(memory_space=pltpu.VMEM)
-    smem = pl.BlockSpec(memory_space=pltpu.SMEM)
     hbm = pl.BlockSpec(memory_space=pl.ANY)
     low = lambda *shape: pltpu.VMEM(shape, BF)
     wide = lambda *shape: pltpu.VMEM(shape, F32)
@@ -615,9 +576,11 @@
             jax.ShapeDtypeStruct((2, slots, chans), BF),
             jax.ShapeDtypeStruct((2, heads, slots), F32),
         ],
-        in_specs=[smem] * 2 + [hbm, vmem] + [hbm] * 5,
-        out_specs=[vmem] * 3,
+        in_specs=[hbm] * 3 + [vmem] + [hbm] * 5,
+        out_specs=[hbm, vmem, vmem],
         scratch_shapes=[
+            pltpu.SMEM(neighbours.shape, jnp.int32),
+            pltpu.SMEM(counts.shape, jnp.int32),
             low(blocks, slots, chans),
             low(9, 2 * heads, slots),
             wide(blocks, heads, slots),
@@ -649,9 +612,7 @@
             low(2, ROWS, chans),
             low(NPEER, ROWS, chans),
             low(2, ROWS, chans),
-        ]
-        + [dma((NPEER,))] * 7 + [dma((2 * NPEER,))] * 3
-        + [
+            low(2 * NPEER, ROWS, chans),
             low(2, 3, slots, chans),
             wide(2, 3, heads, slots),
             low(2, 2, slots, chans),
@@ -659,11 +620,57 @@
             low(2, 2, slots, chans),
             wide(2, 2, heads, slots),
         ]
-        + [dma((4,))] * 4
-        + [dma((7,)), dma((10,)), dma((12,)), dma((8,)), dma((9,))],
-        compiler_params=pltpu.CompilerParams(collective_id=0, has_side_effects=True, vmem_limit_bytes=48 << 20),
+        + [dma((count,)) for count in (7, 2, 5, 5, 3, 3)]
+        + [dma((count,)) for count in (2, 2, 2, 2, 2, 2, 2, 2, 1, 1, 2, 2, 4, 4)],
+        compiler_params=pltpu.CompilerParams(collective_id=0, has_side_effects=True, vmem_limit_bytes=62 << 20),
         name="layer_backward",
     )(neighbours, counts, feat, key_bias, grad_out, w_query, w_key, w_value, w_out)
+
+
+def finish_kernel(scale, low, grad_feat, grad_bias, feat_out, bias_out, w0, w1, w2, w3, packed, plain, load_sem, store_sem):
+    weights = (w0, w1, w2, w3)
+    chans = w0.shape[0]
+    loads = [pltpu.make_async_copy(low.at[pl.ds(chans * i, chans)], packed.at[i], load_sem.at[i]) for i in range(4)]
+    for load in loads:
+        load.start()
+    stores = [
+        pltpu.make_async_copy(grad_feat, feat_out.at[0], store_sem.at[4]),
+        pltpu.make_async_copy(grad_bias, bias_out.at[0], store_sem.at[5]),
+    ]
+    for store in stores:
+        store.start()
+    for i in range(4):
+        loads[i].wait()
+        plain[i] = packed[i].astype(F32) * scale
+        stores.append(pltpu.make_async_copy(plain.at[i], weights[i], store_sem.at[i]))
+        stores[-1].start()
+    for store in stores:
+        store.wait()
+
+
+def finish_call(low, grad_feat, grad_bias, scale):
+    chans = low.shape[1]
+    hbm = pl.BlockSpec(memory_space=pl.ANY)
+    dma = pltpu.SemaphoreType.DMA
+    weight = jax.ShapeDtypeStruct((chans, chans), F32)
+    return pl.pallas_call(
+        functools.partial(finish_kernel, scale),
+        out_shape=[
+            jax.ShapeDtypeStruct((1,) + grad_feat.shape, BF),
+            jax.ShapeDtypeStruct((1,) + grad_bias.shape, F32),
+        ]
+        + [weight] * 4,
+        in_specs=[hbm] * 3,
+        out_specs=[hbm] * 6,
+        scratch_shapes=[
+            pltpu.VMEM((4, chans, chans), BF),
+            pltpu.VMEM((4, chans, chans), F32),
+            dma((4,)),
+            dma((6,)),
+        ],
+        compiler_params=pltpu.CompilerParams(vmem_limit_bytes=62 << 20),
+        name="scale_weights",
+    )(low, grad_feat, grad_bias)
 
 
 def per_device(
@@ -676,14 +683,8 @@
         w_query, w_key, w_value, w_out,
     )
     cells = lax.axis_size("lat") * lax.axis_size("lon") * brows * bcols * slots
-    summed = low.astype(F32).reshape(4, chans, chans) * float(cells) ** (-0.5)
-    return (
-        grad_features.reshape(brows, bcols, slots, chans),
-        grad_bias.reshape(brows, bcols, heads, slots),
-        summed[0],
-        summed[1],
-        summed[2],
-        summed[3],
+    return tuple(
+        finish_call(low.reshape(4 * chans, chans), grad_features, grad_bias, float(cells) ** (-0.5))
     )
 
 

time: 77.9 us -> 68.6 us (0.88)
  local copies, waits for them, and re-layouts: 10.5 us -> 0 us
  Pallas kernels: 66.2 us -> 67.8 us
    unnamed x20 -> x0, local copies, waits for them, and re-layouts: 9.01 us -> none
    pallas_call x0 -> x1, Pallas kernels: none -> 7.41 us  [finish_call(): pl.pallas_call(functools.partial(finish_kernel, scale), out_shape=[jax.Sh...]
    pallas_call x1, Pallas kernels: 66.2 us -> 60.4 us  [layer_call(): pl.pallas_call(layer_kernel, out_shape=[jax.ShapeDtypeStruct((2 * NPEER,...]
    slice x1 -> x0, local copies, waits for them, and re-layouts: 1.44 us -> none  [per_device(): summed[3]]
where the time goes in v3:
time: 68.6 us; the launch traced here: 68.4 us
  Pallas kernels  67.8 us (99%)
    pallas_call x1, Pallas kernels, layer_call(): pl.pallas_call(layer_kernel, out_shape=[jax.ShapeDtypeStruct((2 * NPEER,...  60.4 us
    pallas_call x1, Pallas kernels, finish_call(): pl.pallas_call(functools.partial(finish_kernel, scale), out_shape=[jax.Sh...  7.41 us

profile of v3, /device:TPU:1, one launch (start us, length us, event | category | flops | bytes accessed | tf_op | source)
XLA Modules:
  0.0 68.4 jit_solution(10286002508882612487)
XLA Ops:
  0.6 60.4 %layer_backward.1 = (bf16[48,32,384]{2,1,0:T(8,128)(2,1)}, bf16[2,128,384]{2,1,0:T(8,128)(2,1)}, f32[2,8,128]{2,1,0:T(8,128)}) custom-call(s32[1,2,4]{2,1,0:T(2,128)} %neighbours_hbm.1, s32[1,2,4]{2,1,0:T(2,128)} %counts_hbm.1, bf16[1,2,128,384]{3,2,1,0:T(8,128)(2,1)} %feat.1, bf16[16,128]{1,0:T(8,128)(2,1)} %bitcast.3, bf16[1,2,128,384]{3,2,1,0:T(8,128)(2,1)} %grad_out.1, ...), custom_call_target="tpu_custom_call" | custom-call | tf_op jit(solution)/shard_map/layer_backward/pallas_call | solution.py:572
  61.0 7.4 %scale_weights.1 = (bf16[1,2,128,384]{3,2,1,0:T(8,128)(2,1)}, f32[1,2,8,128]{3,2,1,0:T(8,128)}, f32[384,384]{1,0:T(8,128)}, f32[384,384]{1,0:T(8,128)}, f32[384,384]{1,0:T(8,128)}, /*index=5*/f32[384,384]{1,0:T(8,128)}) custom-call(bf16[1536,384]{1,0:T(8,128)(2,1)} %bitcast.2, bf16[2,128,384]{2,1,0:T(8,128)(2,1)} %get-tuple-element.10.grad_feat, ...), custom_call_target="tpu_custom_call" | custom-call | tf_op jit(solution)/shard_map/scale_weights/pallas_call | solution.py:656

commit v4 on v3

--- a/solution.py
+++ b/solution.py
@@ -45,7 +45,7 @@
 
 
 def attend(
-    neighbours, counts, ext, ext_bias, grad_out, query_all, grad_att_all, key_value, part,
+    neighbours, counts, ext, ext_bias, grad_out, query_all, grad_att_all, key_value, part, send_part,
     w_kv, gathered, scores, grad_probs, probs_low, scores_low, scores_rest, grad_kv,
     attended_t, grad_query_t, bias_parts,
 ):
@@ -173,20 +173,25 @@
     def put(index, value):
         part[index * piece:(index + 1) * piece] = value.astype(BF).reshape(piece, ROWS, chans)
 
-    put(0, mm(feat_both, grad_query, TN))
-    put(3, mm(attended_t[...], grad_both))
     weight_kv = mm(gathered[...].reshape(2 * keys_all, chans), grad_kv[...], TN)
     put(1, weight_kv[:, :chans])
     put(2, weight_kv[:, chans:])
+    send_part(0)
+    put(0, mm(feat_both, grad_query, TN))
+    put(3, mm(attended_t[...], grad_both))
+    send_part(1)
     return all_picks, grad_query
 
 
-def scatter(all_picks, grad_query, w_query, w_kv, grad_kv, bias_parts, feat_parts, halo, own, bias_sum):
+def feature_parts(w_kv, grad_kv, feat_parts):
+    keys_all = feat_parts.shape[1]
+    for b in range(2):
+        feat_parts[b] = mm(grad_kv[pl.ds(b * keys_all, keys_all), :], w_kv[...], NT)
+
+
+def scatter(all_picks, grad_query, w_query, bias_parts, feat_parts, halo, own, bias_sum):
     slots, chans = halo.shape[1:]
     entries = len(all_picks[0])
-    keys_all = entries * slots
-    for b in range(2):
-        feat_parts[b] = mm(grad_kv[pl.ds(b * keys_all, keys_all), :], w_kv[...], NT)
     query_part = mm(grad_query, w_query[...], NT)
     for slot in range(halo.shape[0]):
         column = slot // 3
@@ -214,6 +219,17 @@
 NZ = 8
 NPEER = NXY + NZ
 ROWS = 32
+
+
+def ring(offset, size):
+    return min(offset, size - offset)
+
+
+PLANE = sorted(
+    [(dx, dy) for dx in range(4) for dy in range(4) if dx or dy],
+    key=lambda o: -(ring(o[0], 4) + ring(o[1], 4)),
+)
+DEPTH = sorted(range(1, NZ), key=lambda o: -ring(o, NZ))
 
 
 def remote(src, dst, send_sem, recv_sem, device):
@@ -257,12 +273,18 @@
     off = (lat, off_lon)
     seam = nlat // 2
 
-    def plane_peer(index):
-        x = index // 4
-        return ((x // 2) * 4 + index % 4, (x % 2) * (2 * NZ) + z * 2 + core)
-
-    def depth_peer(index):
-        return (lat, x_lo * (2 * NZ) + index * 2 + core)
+    x = x_hi * 2 + x_lo
+
+    def plane_peers():
+        for dx, dy in PLANE:
+            px = (x + dx) % 4
+            py = (y + dy) % 4
+            yield px * 4 + py, ((px // 2) * 4 + py, (px % 2) * (2 * NZ) + z * 2 + core)
+
+    def depth_peers():
+        for dz in DEPTH:
+            pz = (z + dz) % NZ
+            yield pz, (lat, x_lo * (2 * NZ) + pz * 2 + core)
 
     barrier = pltpu.get_barrier_semaphore()
 
@@ -284,8 +306,6 @@
         (neighbours_hbm, neighbours, 5),
         (counts_hbm, counts, 6),
     ]
-    for src, dst, index in loads:
-        pltpu.make_async_copy(src, dst, local_sem.at[index]).start()
     greet(partner)
     greet(off)
 
@@ -299,19 +319,19 @@
         greet((lat + 1, off_lon))
         greet((lat + 1, partner[1]))
 
-    @pl.loop(1, NXY)
-    def _(step):
-        greet(plane_peer((xy + step) % NXY))
-
-    @pl.loop(1, NZ)
-    def _(step):
-        greet(depth_peer((z + step) % NZ))
+    for src, dst, index in loads:
+        pltpu.make_async_copy(src, dst, local_sem.at[index]).start()
+    for _, device in plane_peers():
+        greet(device)
+    for _, device in depth_peers():
+        greet(device)
 
     near_bias[4] = key_bias[...]
-    settle(ext.at[pl.ds(0, 2)], local_sem.at[0])
     inner = jnp.minimum(lat, 1) + jnp.minimum(nlat - 1 - lat, 1)
     pl.semaphore_wait(barrier, NPEER + 2 * inner)
 
+    feat_off = feat.at[0, core]
+    feat_in = feat.at[0, 1 - core]
     s_off = 4 + 3 * core
     s_in = 7 - 3 * core
     t_off = 9 - 9 * core
@@ -320,7 +340,7 @@
     b_in = 2 * core
 
     def wide_copy(source, target, sent, landed, device):
-        return remote(ext.at[source], ext.at[target], wide_send.at[sent], wide_recv.at[landed], device)
+        return remote(source, ext.at[target], wide_send.at[sent], wide_recv.at[landed], device)
 
     def near_copy(target, sent, landed, device):
         return remote(near_bias.at[4], near_bias.at[target], near_send.at[sent], near_recv.at[landed], device)
@@ -330,21 +350,22 @@
         corner = (lat - 1, off_lon) if up else (lat + 1, off_lon)
         inside = (corner[0], partner[1])
         step, row, sent, landed = (1, 2, 1, 2) if up else (-1, 0, 2, 1)
-        wide_copy(s_in, s_in + step, sent, landed, device).start()
-        wide_copy(s_off, t_off + row, sent, landed + 2, corner).start()
-        wide_copy(s_off, s_off + step, sent, landed + 2, device).start()
+        wide_copy(feat_in, s_in + step, sent, landed, device).start()
+        wide_copy(feat_off, t_off + row, sent, landed + 2, corner).start()
+        wide_copy(feat_off, s_off + step, sent, landed + 2, device).start()
         near_copy(3 * row + 1, sent, landed, device).start()
         near_copy(3 * row + b_off, sent, landed, corner).start()
         near_copy(3 * row + b_in, sent, landed, inside).start()
 
-    wide_copy(s_in, t_in + 1, 0, 0, partner).start()
-    wide_copy(s_off, t_off + 1, 0, 0, off).start()
+    wide_copy(feat_in, t_in + 1, 0, 0, partner).start()
+    wide_copy(feat_off, t_off + 1, 0, 0, off).start()
     near_copy(3 + b_in, 0, 0, partner).start()
     near_copy(3 + b_off, 0, 0, off).start()
     pl.when(lat == seam - 1)(lambda: to_row(False))
     pl.when(lat > 0)(lambda: to_row(True))
     pl.when((lat < nlat - 1) & (lat != seam - 1))(lambda: to_row(False))
 
+    settle(ext.at[pl.ds(0, 2)], local_sem.at[0])
     settle(w_query, local_sem.at[1])
     settle(grad_rows, local_sem.at[2])
     settle(w_out, local_sem.at[3])
@@ -357,7 +378,7 @@
         landed = 1 + row // 2
         slot = s_in - 1 + row
         settle(ext.at[slot], wide_recv.at[landed])
-        wide_copy(slot, t_in + row, landed + 2, landed + 2, partner).start()
+        wide_copy(ext.at[slot], t_in + row, landed + 2, landed + 2, partner).start()
 
     def arrived(row):
         landed = 1 + row // 2
@@ -381,8 +402,19 @@
         ext_bias[6 + row] = own_bias[heads:]
         ext_bias[9 + row] = east_bias[:heads]
 
+    def core_copy(which):
+        start, offset = ((2 - core, core), (3 - 3 * core, 1 - core))[which]
+        count = NPEER // 2
+        return remote(
+            part.at[pl.ds(start * count, count)], from_core.at[pl.ds(offset * count, count)],
+            core_send.at[which], core_recv.at[which], partner,
+        )
+
+    def send_part(which):
+        core_copy(which).start()
+
     all_picks, grad_query = attend(
-        neighbours, counts, ext, ext_bias, grad_rows, query, grad_att, key_value, part,
+        neighbours, counts, ext, ext_bias, grad_rows, query, grad_att, key_value, part, send_part,
         w_kv, gathered, scores, grad_probs, probs_low, scores_low, scores_rest, grad_kv,
         attended_t, grad_query_t, bias_parts,
     )
@@ -390,39 +422,20 @@
     plane = pl.ds(0, NXY)
     depth = pl.ds(NXY, NZ)
 
-    def core_copy(which):
-        start, count = ((0, NXY), (NXY, NZ))[which]
-        return remote(
-            part.at[pl.ds(other + start, count)], from_core.at[pl.ds(start, count)],
-            core_send.at[which], core_recv.at[which], partner,
-        )
-
-    core_copy(1).start()
-    core_copy(0).start()
-
-    def add_core(start, count):
-        mine_rows = part[pl.ds(base + start, count)].astype(F32)
-        half[pl.ds(start, count)] = (mine_rows + from_core[pl.ds(start, count)].astype(F32)).astype(BF)
-
+    feature_parts(w_kv, grad_kv, feat_parts)
+    core_copy(0).wait_recv()
     core_copy(1).wait_recv()
-    add_core(NXY, NZ)
-
-    @pl.loop(1, NZ)
-    def _(step):
-        peer = (z + step) % NZ
-        remote(half.at[NXY + peer], from_first.at[NXY + z], first_send.at[1], first_recv.at[1], depth_peer(peer)).start()
-
-    core_copy(0).wait_recv()
-    add_core(0, NXY)
-
-    @pl.loop(1, NXY)
-    def _(step):
-        peer = (xy + step) % NXY
-        remote(half.at[peer], from_first.at[xy], first_send.at[0], first_recv.at[0], plane_peer(peer)).start()
+    half[...] = (part[pl.ds(base, NPEER)].astype(F32) + from_core[...].astype(F32)).astype(BF)
+
+    for peer, device in depth_peers():
+        remote(half.at[NXY + peer], from_first.at[NXY + z], first_send.at[1], first_recv.at[1], device).start()
+
+    for peer, device in plane_peers():
+        remote(half.at[peer], from_first.at[xy], first_send.at[0], first_recv.at[0], device).start()
 
     from_first[xy] = half[xy]
     from_first[NXY + z] = half[NXY + z]
-    scatter(all_picks, grad_query, w_query, w_kv, grad_kv, bias_parts, feat_parts, halo, own, bias_sum)
+    scatter(all_picks, grad_query, w_query, bias_parts, feat_parts, halo, own, bias_sum)
     for index in range(2):
         device = (west, east)[index]
         columns = pl.ds(9 * index, 3)
@@ -432,29 +445,17 @@
     settle(half.at[pl.ds(0, NZ - 1)], first_recv.at[1])
     mine[1] = jnp.sum(from_first[depth].astype(F32), axis=0).astype(BF)
 
-    @pl.loop(1, NXY)
-    def _(step):
-        peer = (xy + step) % NXY
-        remote(mine.at[1], from_second.at[xy], second_send.at[1], second_recv.at[1], plane_peer(peer)).start()
+    for peer, device in plane_peers():
+        remote(mine.at[1], from_second.at[xy], second_send.at[1], second_recv.at[1], device).start()
 
     settle(half.at[pl.ds(0, NXY - 1)], first_recv.at[0])
     mine[0] = jnp.sum(from_first[plane].astype(F32), axis=0).astype(BF)
 
-    @pl.loop(1, NZ)
-    def _(step):
-        peer = (z + step) % NZ
-        remote(mine.at[0], from_second.at[NXY + z], second_send.at[0], second_recv.at[0], depth_peer(peer)).start()
+    for peer, device in depth_peers():
+        remote(mine.at[0], from_second.at[NXY + z], second_send.at[0], second_recv.at[0], device).start()
 
     from_second[xy] = mine[1]
     from_second[NXY + z] = mine[0]
-
-    settle(side, side_recv.at[0])
-    settle(side_bias, side_recv.at[1])
-    for index in range(2):
-        for j in range(2):
-            slot = 3 * j + 3 + 2 * index
-            rows_out[index, j] = (halo[slot].astype(F32) + side[j, 2 * index].astype(F32)).astype(BF)
-            rows_bias[index, j] = bias_sum[slot] + side_bias[j, 2 * index]
 
     def to_edge(index):
         device = (north, south)[index]
@@ -462,41 +463,49 @@
         remote(rows_out.at[index], edge.at[1 - index], edge_send.at[2 * index], edge_recv.at[landed], device).start()
         remote(rows_bias.at[index], edge_bias.at[1 - index], edge_send.at[2 * index + 1], edge_recv.at[landed + 1], device).start()
 
-    pl.when(lat == seam - 1)(lambda: to_edge(1))
-    pl.when(lat > 0)(lambda: to_edge(0))
-    pl.when((lat < nlat - 1) & (lat != seam - 1))(lambda: to_edge(1))
+    def fold_columns():
+        settle(side, side_recv.at[0])
+        settle(side_bias, side_recv.at[1])
+        for index in range(2):
+            for j in range(2):
+                slot = 3 * j + 3 + 2 * index
+                rows_out[index, j] = (halo[slot].astype(F32) + side[j, 2 * index].astype(F32)).astype(BF)
+                rows_bias[index, j] = bias_sum[slot] + side_bias[j, 2 * index]
+        pl.when(lat == seam - 1)(lambda: to_edge(1))
+        pl.when(lat > 0)(lambda: to_edge(0))
+        pl.when((lat < nlat - 1) & (lat != seam - 1))(lambda: to_edge(1))
+
+    wraps = (z == (NZ - 1) * core)
+    pl.when(jnp.logical_not(wraps))(fold_columns)
 
     settle(half.at[pl.ds(0, NXY - 1)], second_recv.at[1])
     total[1] = jnp.sum(from_second[plane].astype(F32), axis=0).astype(BF)
 
-    @pl.loop(1, NZ)
-    def _(step):
-        peer = (z + step) % NZ
-        remote(total.at[1], summed.at[base + NXY + z], third_send.at[1], third_recv.at[1], depth_peer(peer)).start()
-
-    summed[base + NXY + z] = total[1]
+    for peer, device in depth_peers():
+        remote(total.at[1], summed.at[NXY + z], third_send.at[1], third_recv.at[1], device).start()
+
+    summed[NXY + z] = total[1]
+    pl.when(wraps)(fold_columns)
     settle(half.at[pl.ds(0, NZ - 1)], second_recv.at[0])
     total[0] = jnp.sum(from_second[depth].astype(F32), axis=0).astype(BF)
 
-    @pl.loop(1, NXY)
-    def _(step):
-        peer = (xy + step) % NXY
-        remote(total.at[0], summed.at[base + xy], third_send.at[0], third_recv.at[0], plane_peer(peer)).start()
-
-    summed[base + xy] = total[0]
+    for peer, device in plane_peers():
+        remote(total.at[0], summed.at[xy], third_send.at[0], third_recv.at[0], device).start()
+
+    summed[xy] = total[0]
 
     def fourth_copy(which):
         start, count = ((0, NXY), (NXY, NZ))[which]
-        rows = summed.at[pl.ds(base + start, count)]
-        return remote(rows, rows, fourth_send.at[0], fourth_recv.at[0], partner)
+        return remote(
+            summed.at[pl.ds(start, count)], out.at[pl.ds(base + start, count)],
+            fourth_send.at[0], fourth_recv.at[0], partner,
+        )
 
     settle(half.at[pl.ds(0, NZ - 1)], third_recv.at[1])
     fourth_copy(1).start()
     settle(half.at[pl.ds(0, NXY - 1)], third_recv.at[0])
     fourth_copy(0).start()
-    own_rows = pl.ds(base, NPEER)
-    other_rows = pl.ds(other, NPEER)
-    own_out = pltpu.make_async_copy(summed.at[own_rows], out.at[own_rows], out_sem.at[0])
+    own_out = pltpu.make_async_copy(summed, out.at[pl.ds(base, NPEER)], out_sem.at[0])
     own_out.start()
 
     @pl.when(lat == 0)
@@ -552,10 +561,7 @@
         settle(half.at[pl.ds(0, NZ - 1)], sems.at[1 - wide_index])
     settle(half, fourth_send.at[0])
     settle(half, fourth_recv.at[0])
-    other_out = pltpu.make_async_copy(summed.at[other_rows], out.at[other_rows], out_sem.at[1])
-    other_out.start()
     own_out.wait()
-    other_out.wait()
 
 
 def layer_call(neighbours, counts, feat, key_bias, grad_out, w_query, w_key, w_value, w_out):
@@ -612,7 +618,7 @@
             low(2, ROWS, chans),
             low(NPEER, ROWS, chans),
             low(2, ROWS, chans),
-            low(2 * NPEER, ROWS, chans),
+            low(NPEER, ROWS, chans),
             low(2, 3, slots, chans),
             wide(2, 3, heads, slots),
             low(2, 2, slots, chans),
@@ -620,30 +626,32 @@
             low(2, 2, slots, chans),
             wide(2, 2, heads, slots),
         ]
-        + [dma((count,)) for count in (7, 2, 5, 5, 3, 3)]
+        + [dma((count,)) for count in (7, 1, 5, 5, 3, 3)]
         + [dma((count,)) for count in (2, 2, 2, 2, 2, 2, 2, 2, 1, 1, 2, 2, 4, 4)],
         compiler_params=pltpu.CompilerParams(collective_id=0, has_side_effects=True, vmem_limit_bytes=62 << 20),
         name="layer_backward",
     )(neighbours, counts, feat, key_bias, grad_out, w_query, w_key, w_value, w_out)
 
 
-def finish_kernel(scale, low, grad_feat, grad_bias, feat_out, bias_out, w0, w1, w2, w3, packed, plain, load_sem, store_sem):
+def finish_kernel(
+    scale, low, grad_feat, grad_bias, feat_out, bias_out, w0, w1, w2, w3,
+    packed, plain, feat_rows, bias_rows, load_sem, store_sem,
+):
     weights = (w0, w1, w2, w3)
     chans = w0.shape[0]
-    loads = [pltpu.make_async_copy(low.at[pl.ds(chans * i, chans)], packed.at[i], load_sem.at[i]) for i in range(4)]
+    loads = [(low.at[pl.ds(chans * i, chans)], packed.at[i]) for i in range(4)]
+    loads += [(grad_feat, feat_rows), (grad_bias, bias_rows)]
+    loads = [pltpu.make_async_copy(src, dst, load_sem.at[i]) for i, (src, dst) in enumerate(loads)]
     for load in loads:
         load.start()
-    stores = [
-        pltpu.make_async_copy(grad_feat, feat_out.at[0], store_sem.at[4]),
-        pltpu.make_async_copy(grad_bias, bias_out.at[0], store_sem.at[5]),
-    ]
-    for store in stores:
-        store.start()
-    for i in range(4):
+    stores = [(plain.at[i], weights[i]) for i in range(4)]
+    stores += [(feat_rows, feat_out.at[0]), (bias_rows, bias_out.at[0])]
+    stores = [pltpu.make_async_copy(src, dst, store_sem.at[i]) for i, (src, dst) in enumerate(stores)]
+    for i in range(6):
         loads[i].wait()
-        plain[i] = packed[i].astype(F32) * scale
-        stores.append(pltpu.make_async_copy(plain.at[i], weights[i], store_sem.at[i]))
-        stores[-1].start()
+        if i < 4:
+            plain[i] = packed[i].astype(F32) * scale
+        stores[i].start()
     for store in stores:
         store.wait()
 
@@ -665,7 +673,9 @@
         scratch_shapes=[
             pltpu.VMEM((4, chans, chans), BF),
             pltpu.VMEM((4, chans, chans), F32),
-            dma((4,)),
+            pltpu.VMEM(grad_feat.shape, BF),
+            pltpu.VMEM(grad_bias.shape, F32),
+            dma((6,)),
             dma((6,)),
         ],
         compiler_params=pltpu.CompilerParams(vmem_limit_bytes=62 << 20),

time: 68.6 us -> 63 us (0.918)
  Pallas kernels: 67.8 us -> 62.3 us
    pallas_call x1, Pallas kernels: 7.41 us -> 2.56 us  [finish_call(): pl.pallas_call(functools.partial(finish_kernel, scale), out_shape=[jax.Sh...]
where the time goes in v4:
time: 63 us; the launch traced here: 62.9 us
  Pallas kernels  62.3 us (99%)
  between operations  0.64 us (1%)
    pallas_call x1, Pallas kernels, layer_call(): pl.pallas_call(layer_kernel, out_shape=[jax.ShapeDtypeStruct((2 * NPEER,...  59.7 us
    pallas_call x1, Pallas kernels, finish_call(): pl.pallas_call(functools.partial(finish_kernel, scale), out_shape=[jax.Sh...  2.56 us

profile of v4, /device:TPU:1, one launch (start us, length us, event | category | flops | bytes accessed | tf_op | source)
XLA Modules:
  0.0 62.9 jit_solution(8652806828724926405)
XLA Ops:
  0.6 59.7 %layer_backward.1 = (bf16[48,32,384]{2,1,0:T(8,128)(2,1)}, bf16[2,128,384]{2,1,0:T(8,128)(2,1)}, f32[2,8,128]{2,1,0:T(8,128)}) custom-call(s32[1,2,4]{2,1,0:T(2,128)} %neighbours_hbm.1, s32[1,2,4]{2,1,0:T(2,128)} %counts_hbm.1, bf16[1,2,128,384]{3,2,1,0:T(8,128)(2,1)} %feat.1, bf16[16,128]{1,0:T(8,128)(2,1)} %bitcast.3, bf16[1,2,128,384]{3,2,1,0:T(8,128)(2,1)} %grad_out.1, ...), custom_call_target="tpu_custom_call" | custom-call | tf_op jit(solution)/shard_map/layer_backward/pallas_call | solution.py:578
  60.3 2.6 %scale_weights.1 = (bf16[1,2,128,384]{3,2,1,0:T(8,128)(2,1)}, f32[1,2,8,128]{3,2,1,0:T(8,128)}, f32[384,384]{1,0:T(8,128)}, f32[384,384]{1,0:T(8,128)}, f32[384,384]{1,0:T(8,128)}, /*index=5*/f32[384,384]{1,0:T(8,128)}) custom-call(bf16[1536,384]{1,0:T(8,128)(2,1)} %bitcast.2, bf16[2,128,384]{2,1,0:T(8,128)(2,1)} %get-tuple-element.10.grad_feat, ...), custom_call_target="tpu_custom_call" | custom-call | tf_op jit(solution)/shard_map/scale_weights/pallas_call | solution.py:664

commit v5 on v4

--- a/solution.py
+++ b/solution.py
@@ -46,7 +46,7 @@
 
 def attend(
     neighbours, counts, ext, ext_bias, grad_out, query_all, grad_att_all, key_value, part, send_part,
-    w_kv, gathered, scores, grad_probs, probs_low, scores_low, scores_rest, grad_kv,
+    w_kv, gathered, scores, grad_probs, probs_low, scores_low, grad_kv,
     attended_t, grad_query_t, bias_parts,
 ):
     lat = lax.axis_index("lat")
@@ -69,14 +69,12 @@
     row = lax.broadcasted_iota(jnp.int32, (slots, WINDOW), 0)
     place_row = lax.broadcasted_iota(jnp.int32, (HEADS, WINDOW), 0)
     place_lane = lax.broadcasted_iota(jnp.int32, (HEADS, WINDOW), 1)
-    pick_row = lax.broadcasted_iota(jnp.int32, (2 * HEADS, PAIR * slots), 0)
-    pick_lane = lax.broadcasted_iota(jnp.int32, (2 * HEADS, PAIR * slots), 1)
-    all_picks = []
-    for b in range(2):
+    wide_lane = lax.broadcasted_iota(jnp.int32, (keys_all, slots), 1)
+    bias_all = [jnp.zeros((keys_all, slots), F32)] * 2
+    state = {}
+
+    def gather(b):
         picks = [local_slot(neighbours[0, b, e]) for e in range(entries)]
-        all_picks.append(picks)
-        query = query_all[b]
-        grad_att = grad_att_all[b]
         gathered[b, 0:slots, :] = ext[3 * b + 4]
         for e in range(1, entries):
             gathered[b, e * slots:(e + 1) * slots, :] = ext[picks[e]]
@@ -84,87 +82,110 @@
         key_value[rest, :] = mm(gathered[b, slots:], w_kv[...]).astype(BF)
         kv = key_value[pl.ds(b * keys_all, keys_all), :]
         bias_row = jnp.concatenate([ext_bias[picks[e]] for e in range(entries)], axis=1)
-        bias_rows = jnp.zeros((2 * HEADS, keys_all), F32)
-        for w in range(2):
-            lo = w * (chans - WINDOW)
-            first = PAIR * w
-            spare = PAIR * width if w == 0 else 0
-            region = (lane < PAIR * width) if w == 0 else (lane >= WINDOW - PAIR * width)
-            place = jnp.zeros((HEADS, WINDOW), F32)
-            for hh in range(PAIR):
-                start = spare + 3 * hh
-                place = jnp.where(
-                    (place_row == first + hh) & (place_lane >= start) & (place_lane < start + 3), 1.0, place
-                )
-            bias_cols = mm(bias_row, place, TN)
-            key_aug = []
-            for e in range(entries):
-                cols = bias_cols[e * slots:(e + 1) * slots]
-                cols = jnp.where((lane == spare + 3 * PAIR) & (row >= counts[0, b, e]), FAR, cols)
-                piece = kv[e * slots:(e + 1) * slots, lo:lo + WINDOW]
-                key_aug.append(jnp.where(region, piece.astype(F32), cols).astype(BF))
-            key_aug = jnp.concatenate(key_aug, axis=0)
-            value_win = kv[:, chans + lo:chans + lo + WINDOW]
-            query_win = query[:, lo:lo + WINDOW].astype(F32)
-            grad_win = grad_att[:, lo:lo + WINDOW].astype(F32)
-            query_aug, grad_aug = [], []
-            for hh in range(PAIR):
-                inside = (lane >= (first + hh) * width - lo) & (lane < (first + hh + 1) * width - lo)
-                const = jnp.where(lane == spare + 3 * PAIR, 1.0, 0.0)
-                for t in range(3):
-                    const = jnp.where(lane == spare + 3 * hh + t, parts[t], const)
-                query_aug.append(jnp.where(inside, query_win, const).astype(BF))
-                grad_aug.append(jnp.where(inside, grad_win, 0.0).astype(BF))
-            query_aug = jnp.concatenate(query_aug, axis=0)
-            grad_aug = jnp.concatenate(grad_aug, axis=0)
-            scores[...] = mm(key_aug, query_aug, NT)
-            grad_probs[...] = mm(value_win, grad_aug, NT)
-            for hh in range(PAIR):
-                cut = pl.ds(hh * slots, slots)
-                logits = scores[:, cut]
-                powers = jnp.exp2((logits - jnp.max(logits, axis=0, keepdims=True)) * log2e)
-                probs = powers * (1.0 / jnp.sum(powers, axis=0, keepdims=True))
-                probs_low[:, cut] = probs.astype(BF)
-                grads = grad_probs[:, cut]
-                centre = jnp.sum(probs * grads, axis=0, keepdims=True)
-                full = probs * (grads - centre)
-                high = full.astype(BF)
-                scores_low[:, cut] = high
-                scores_rest[:, cut] = (full - high.astype(F32)).astype(BF)
-            value_grad = mm(probs_low[...], grad_aug)
-            key_grad = mm(scores_low[...], query_aug)
-            chosen = jnp.where(pick_lane // slots + first == pick_row, 1.0, 0.0).astype(BF)
-            bias_rows = bias_rows + mm(chosen, scores_low[...], NT) + mm(chosen, scores_rest[...], NT)
-            scale = 1.0 / root
-            base = b * keys_all
-            rows = pl.ds(base, keys_all)
-            half = WINDOW // 2
-            edge = PAIR * width - half
-            low_lane = lane[0:1, 0:half]
-            if w == 0:
-                grad_kv[rows, 0:half] = (key_grad[:, 0:half] * scale).astype(BF)
-                grad_kv[rows, chans:chans + half] = value_grad[:, 0:half].astype(BF)
-                saved_key, saved_value = key_grad[:, half:], value_grad[:, half:]
-            else:
-                middle = jnp.where(low_lane < edge, saved_key, key_grad[:, 0:half]) * scale
-                grad_kv[rows, half:2 * half] = middle.astype(BF)
-                grad_kv[rows, 2 * half:3 * half] = (key_grad[:, half:] * scale).astype(BF)
-                middle = saved_value + value_grad[:, 0:half]
-                grad_kv[rows, chans + half:chans + 2 * half] = middle.astype(BF)
-                grad_kv[rows, chans + 2 * half:chans + 3 * half] = value_grad[:, half:].astype(BF)
-            for pair in range(2):
-                head = first + 2 * pair
-                cut = pl.ds(2 * pair * slots, 2 * slots)
-                value_rows = kv[:, chans + head * width:chans + (head + 2) * width]
-                key_rows = kv[:, head * width:(head + 2) * width]
-                both = mm(value_rows, probs_low[:, cut], TN)
-                attended_t[head * width:(head + 1) * width, b * slots:(b + 1) * slots] = both[:width, :slots].astype(BF)
-                attended_t[(head + 1) * width:(head + 2) * width, b * slots:(b + 1) * slots] = both[width:, slots:].astype(BF)
-                both = mm(key_rows, scores_low[:, cut], TN) * scale
-                grad_query_t[head * width:(head + 1) * width, b * slots:(b + 1) * slots] = both[:width, :slots].astype(BF)
-                grad_query_t[(head + 1) * width:(head + 2) * width, b * slots:(b + 1) * slots] = both[width:, slots:].astype(BF)
+        return picks, query_all[b], grad_att_all[b], kv, bias_row
+
+    def prepare(b, w):
+        picks, query, grad_att, kv, bias_row = state[b]
+        lo = w * (chans - WINDOW)
+        first = PAIR * w
+        spare = PAIR * width if w == 0 else 0
+        region = (lane < PAIR * width) if w == 0 else (lane >= WINDOW - PAIR * width)
+        place = jnp.zeros((HEADS, WINDOW), F32)
+        for hh in range(PAIR):
+            start = spare + 3 * hh
+            place = jnp.where(
+                (place_row == first + hh) & (place_lane >= start) & (place_lane < start + 3), 1.0, place
+            )
+        bias_cols = mm(bias_row, place, TN)
+        key_aug = []
         for e in range(entries):
-            bias_parts[b, e] = bias_rows[:HEADS, e * slots:(e + 1) * slots]
+            cols = bias_cols[e * slots:(e + 1) * slots]
+            cols = jnp.where((lane == spare + 3 * PAIR) & (row >= counts[0, b, e]), FAR, cols)
+            piece = kv[e * slots:(e + 1) * slots, lo:lo + WINDOW]
+            key_aug.append(jnp.where(region, piece.astype(F32), cols).astype(BF))
+        key_aug = jnp.concatenate(key_aug, axis=0)
+        value_win = kv[:, chans + lo:chans + lo + WINDOW]
+        query_win = query[:, lo:lo + WINDOW].astype(F32)
+        grad_win = grad_att[:, lo:lo + WINDOW].astype(F32)
+        query_aug, grad_aug = [], []
+        for hh in range(PAIR):
+            inside = (lane >= (first + hh) * width - lo) & (lane < (first + hh + 1) * width - lo)
+            const = jnp.where(lane == spare + 3 * PAIR, 1.0, 0.0)
+            for t in range(3):
+                const = jnp.where(lane == spare + 3 * hh + t, parts[t], const)
+            query_aug.append(jnp.where(inside, query_win, const).astype(BF))
+            grad_aug.append(jnp.where(inside, grad_win, 0.0).astype(BF))
+        query_aug = jnp.concatenate(query_aug, axis=0)
+        grad_aug = jnp.concatenate(grad_aug, axis=0)
+        scores[2 * b + w] = mm(key_aug, query_aug, NT)
+        grad_probs[2 * b + w] = mm(value_win, grad_aug, NT)
+        return query_aug, grad_aug, lo, first, spare, region
+
+    def soften(b, w):
+        first = PAIR * w
+        bias_sums = bias_all[b]
+        for hh in range(PAIR):
+            cut = pl.ds(hh * slots, slots)
+            logits = scores[2 * b + w, :, cut]
+            powers = jnp.exp2((logits - jnp.max(logits, axis=0, keepdims=True)) * log2e)
+            probs = powers * (1.0 / jnp.sum(powers, axis=0, keepdims=True))
+            probs_low[2 * b + w, :, cut] = probs.astype(BF)
+            grads = grad_probs[2 * b + w, :, cut]
+            centre = jnp.sum(probs * grads, axis=0, keepdims=True)
+            full = probs * (grads - centre)
+            high = full.astype(BF)
+            scores_low[2 * b + w, :, cut] = high
+            bias_sums = jnp.where(wide_lane == first + hh, jnp.sum(full, axis=1, keepdims=True), bias_sums)
+        bias_all[b] = bias_sums
+
+    def finish(b, w):
+        picks, query, grad_att, kv, bias_row = state[b]
+        query_aug, grad_aug, lo, first, spare, region = state[b, w]
+        value_grad = mm(probs_low[2 * b + w], grad_aug)
+        key_grad = mm(scores_low[2 * b + w], query_aug)
+        scale = 1.0 / root
+        base = b * keys_all
+        rows = pl.ds(base, keys_all)
+        half = WINDOW // 2
+        edge = PAIR * width - half
+        low_lane = lane[0:1, 0:half]
+        if w == 0:
+            grad_kv[rows, 0:half] = (key_grad[:, 0:half] * scale).astype(BF)
+            grad_kv[rows, chans:chans + half] = value_grad[:, 0:half].astype(BF)
+            state[b, 'saved'] = key_grad[:, half:], value_grad[:, half:]
+        else:
+            saved_key, saved_value = state[b, 'saved']
+            middle = jnp.where(low_lane < edge, saved_key, key_grad[:, 0:half]) * scale
+            grad_kv[rows, half:2 * half] = middle.astype(BF)
+            grad_kv[rows, 2 * half:3 * half] = (key_grad[:, half:] * scale).astype(BF)
+            middle = saved_value + value_grad[:, 0:half]
+            grad_kv[rows, chans + half:chans + 2 * half] = middle.astype(BF)
+            grad_kv[rows, chans + 2 * half:chans + 3 * half] = value_grad[:, half:].astype(BF)
+        for pair in range(2):
+            head = first + 2 * pair
+            cut = pl.ds(2 * pair * slots, 2 * slots)
+            value_rows = kv[:, chans + head * width:chans + (head + 2) * width]
+            key_rows = kv[:, head * width:(head + 2) * width]
+            both = mm(value_rows, probs_low[2 * b + w, :, cut], TN)
+            attended_t[head * width:(head + 1) * width, b * slots:(b + 1) * slots] = both[:width, :slots].astype(BF)
+            attended_t[(head + 1) * width:(head + 2) * width, b * slots:(b + 1) * slots] = both[width:, slots:].astype(BF)
+            both = mm(key_rows, scores_low[2 * b + w, :, cut], TN) * scale
+            grad_query_t[head * width:(head + 1) * width, b * slots:(b + 1) * slots] = both[:width, :slots].astype(BF)
+            grad_query_t[(head + 1) * width:(head + 2) * width, b * slots:(b + 1) * slots] = both[width:, slots:].astype(BF)
+
+    steps = [(0, 0), (0, 1), (1, 0), (1, 1)]
+    state[0] = gather(0)
+    state[0, 0] = prepare(0, 0)
+    state[1] = gather(1)
+    for i, step in enumerate(steps):
+        if i + 1 < len(steps):
+            state[steps[i + 1]] = prepare(*steps[i + 1])
+        soften(*step)
+        finish(*step)
+    all_picks = [state[b][0] for b in range(2)]
+    for b in range(2):
+        for e in range(entries):
+            bias_parts[b, e] = jnp.transpose(bias_all[b][e * slots:(e + 1) * slots])[:HEADS]
     grad_query = jnp.transpose(grad_query_t[...].astype(F32)).astype(BF)
     feat_both = jnp.concatenate([ext[4], ext[7]], axis=0)
     grad_both = grad_out[...].reshape(2 * slots, chans)
@@ -244,7 +265,7 @@
     out, grad_feat, grad_bias,
     neighbours, counts, ext, near_bias, ext_bias, grad_rows, w_query, w_out, query, grad_att, key_value,
     part, halo, own, bias_sum, feat_parts, bias_parts, w_kv, gathered, scores, grad_probs, probs_low,
-    scores_low, scores_rest, grad_kv, attended_t, grad_query_t,
+    scores_low, grad_kv, attended_t, grad_query_t,
     from_core, half, from_first, mine, from_second, total, summed,
     side, side_bias, rows_out, rows_bias, edge, edge_bias,
     local_sem, out_sem, wide_send, wide_recv, near_send, near_recv,
@@ -415,7 +436,7 @@
 
     all_picks, grad_query = attend(
         neighbours, counts, ext, ext_bias, grad_rows, query, grad_att, key_value, part, send_part,
-        w_kv, gathered, scores, grad_probs, probs_low, scores_low, scores_rest, grad_kv,
+        w_kv, gathered, scores, grad_probs, probs_low, scores_low, grad_kv,
         attended_t, grad_query_t, bias_parts,
     )
 
@@ -604,11 +625,10 @@
             wide(2, entries, heads, slots),
             low(chans, 2 * chans),
             low(2, keys_all, chans),
-            wide(keys_all, PAIR * slots),
-            wide(keys_all, PAIR * slots),
-            low(keys_all, PAIR * slots),
-            low(keys_all, PAIR * slots),
-            low(keys_all, PAIR * slots),
+            wide(4, keys_all, PAIR * slots),
+            wide(4, keys_all, PAIR * slots),
+            low(4, keys_all, PAIR * slots),
+            low(4, keys_all, PAIR * slots),
             low(2 * keys_all, 2 * chans),
             low(chans, 2 * slots),
             low(chans, 2 * slots),

time: 63 us -> 61 us (0.968)
  Pallas kernels: 62.3 us -> 60.2 us
    pallas_call x1, Pallas kernels: 59.7 us -> 57.6 us  [layer_call(): pl.pallas_call(layer_kernel, out_shape=[jax.ShapeDtypeStruct((2 * NPEER,...]
where the time goes in v5:
time: 61 us; the launch traced here: 60.9 us
  Pallas kernels  60.2 us (99%)
  between operations  0.64 us (1%)
    pallas_call x1, Pallas kernels, layer_call(): pl.pallas_call(layer_kernel, out_shape=[jax.ShapeDtypeStruct((2 * NPEER,...  57.6 us
    pallas_call x1, Pallas kernels, finish_call(): pl.pallas_call(functools.partial(finish_kernel, scale), out_shape=[jax.Sh...  2.56 us

profile of v5, /device:TPU:1, one launch (start us, length us, event | category | flops | bytes accessed | tf_op | source)
XLA Modules:
  0.0 60.9 jit_solution(16819771963032632693)
XLA Ops:
  0.6 57.6 %layer_backward.1 = (bf16[48,32,384]{2,1,0:T(8,128)(2,1)}, bf16[2,128,384]{2,1,0:T(8,128)(2,1)}, f32[2,8,128]{2,1,0:T(8,128)}) custom-call(s32[1,2,4]{2,1,0:T(2,128)} %neighbours_hbm.1, s32[1,2,4]{2,1,0:T(2,128)} %counts_hbm.1, bf16[1,2,128,384]{3,2,1,0:T(8,128)(2,1)} %feat.1, bf16[16,128]{1,0:T(8,128)(2,1)} %bitcast.3, bf16[1,2,128,384]{3,2,1,0:T(8,128)(2,1)} %grad_out.1, ...), custom_call_target="tpu_custom_call" | custom-call | tf_op jit(solution)/shard_map/layer_backward/pallas_call | solution.py:599
  58.3 2.6 %scale_weights.1 = (bf16[1,2,128,384]{3,2,1,0:T(8,128)(2,1)}, f32[1,2,8,128]{3,2,1,0:T(8,128)}, f32[384,384]{1,0:T(8,128)}, f32[384,384]{1,0:T(8,128)}, f32[384,384]{1,0:T(8,128)}, /*index=5*/f32[384,384]{1,0:T(8,128)}) custom-call(bf16[1536,384]{1,0:T(8,128)(2,1)} %bitcast.2, bf16[2,128,384]{2,1,0:T(8,128)(2,1)} %get-tuple-element.10.grad_feat, ...), custom_call_target="tpu_custom_call" | custom-call | tf_op jit(solution)/shard_map/scale_weights/pallas_call | solution.py:684

commit v6 on v5

--- a/solution.py
+++ b/solution.py
@@ -506,7 +506,6 @@
         remote(total.at[1], summed.at[NXY + z], third_send.at[1], third_recv.at[1], device).start()
 
     summed[NXY + z] = total[1]
-    pl.when(wraps)(fold_columns)
     settle(half.at[pl.ds(0, NZ - 1)], second_recv.at[0])
     total[0] = jnp.sum(from_second[depth].astype(F32), axis=0).astype(BF)
 
@@ -514,6 +513,7 @@
         remote(total.at[0], summed.at[xy], third_send.at[0], third_recv.at[0], device).start()
 
     summed[xy] = total[0]
+    pl.when(wraps)(fold_columns)
 
     def fourth_copy(which):
         start, count = ((0, NXY), (NXY, NZ))[which]

time: 61 us -> 58.6 us (0.961)
  Pallas kernels: 60.2 us -> 57.8 us
    pallas_call x1, Pallas kernels: 57.6 us -> 55.2 us  [layer_call(): pl.pallas_call(layer_kernel, out_shape=[jax.ShapeDtypeStruct((2 * NPEER,...]
where the time goes in v6:
time: 58.6 us; the launch traced here: 58.4 us
  Pallas kernels  57.8 us (99%)
  between operations  0.64 us (1%)
    pallas_call x1, Pallas kernels, layer_call(): pl.pallas_call(layer_kernel, out_shape=[jax.ShapeDtypeStruct((2 * NPEER,...  55.2 us
    pallas_call x1, Pallas kernels, finish_call(): pl.pallas_call(functools.partial(finish_kernel, scale), out_shape=[jax.Sh...  2.56 us

profile of v6, /device:TPU:1, one launch (start us, length us, event | category | flops | bytes accessed | tf_op | source)
XLA Modules:
  0.0 58.4 jit_solution(11446815097034404479)
XLA Ops:
  0.6 55.2 %layer_backward.1 = (bf16[48,32,384]{2,1,0:T(8,128)(2,1)}, bf16[2,128,384]{2,1,0:T(8,128)(2,1)}, f32[2,8,128]{2,1,0:T(8,128)}) custom-call(s32[1,2,4]{2,1,0:T(2,128)} %neighbours_hbm.1, s32[1,2,4]{2,1,0:T(2,128)} %counts_hbm.1, bf16[1,2,128,384]{3,2,1,0:T(8,128)(2,1)} %feat.1, bf16[16,128]{1,0:T(8,128)(2,1)} %bitcast.3, bf16[1,2,128,384]{3,2,1,0:T(8,128)(2,1)} %grad_out.1, ...), custom_call_target="tpu_custom_call" | custom-call | tf_op jit(solution)/shard_map/layer_backward/pallas_call | solution.py:599
  55.9 2.6 %scale_weights.1 = (bf16[1,2,128,384]{3,2,1,0:T(8,128)(2,1)}, f32[1,2,8,128]{3,2,1,0:T(8,128)}, f32[384,384]{1,0:T(8,128)}, f32[384,384]{1,0:T(8,128)}, f32[384,384]{1,0:T(8,128)}, /*index=5*/f32[384,384]{1,0:T(8,128)}) custom-call(bf16[1536,384]{1,0:T(8,128)(2,1)} %bitcast.2, bf16[2,128,384]{2,1,0:T(8,128)(2,1)} %get-tuple-element.10.grad_feat, ...), custom_call_target="tpu_custom_call" | custom-call | tf_op jit(solution)/shard_map/scale_weights/pallas_call | solution.py:684

commit v7 on v6

--- a/solution.py
+++ b/solution.py
@@ -378,12 +378,13 @@
         near_copy(3 * row + b_off, sent, landed, corner).start()
         near_copy(3 * row + b_in, sent, landed, inside).start()
 
+    pl.when(lat == seam - 1)(lambda: to_row(False))
+    pl.when(lat == seam)(lambda: to_row(True))
     wide_copy(feat_in, t_in + 1, 0, 0, partner).start()
     wide_copy(feat_off, t_off + 1, 0, 0, off).start()
     near_copy(3 + b_in, 0, 0, partner).start()
     near_copy(3 + b_off, 0, 0, off).start()
-    pl.when(lat == seam - 1)(lambda: to_row(False))
-    pl.when(lat > 0)(lambda: to_row(True))
+    pl.when((lat > 0) & (lat != seam))(lambda: to_row(True))
     pl.when((lat < nlat - 1) & (lat != seam - 1))(lambda: to_row(False))
 
     settle(ext.at[pl.ds(0, 2)], local_sem.at[0])

time: 58.6 us -> 58.5 us (level)
  no operation moved by 1% of the time
where the time goes in v7:
time: 58.5 us; the launch traced here: 58.3 us
  Pallas kernels  57.7 us (99%)
  between operations  0.64 us (1%)
    pallas_call x1, Pallas kernels, layer_call(): pl.pallas_call(layer_kernel, out_shape=[jax.ShapeDtypeStruct((2 * NPEER,...  55.1 us
    pallas_call x1, Pallas kernels, finish_call(): pl.pallas_call(functools.partial(finish_kernel, scale), out_shape=[jax.Sh...  2.56 us

profile of v7, /device:TPU:1, one launch (start us, length us, event | category | flops | bytes accessed | tf_op | source)
XLA Modules:
  0.0 58.3 jit_solution(10997248773092480861)
XLA Ops:
  0.6 55.1 %layer_backward.1 = (bf16[48,32,384]{2,1,0:T(8,128)(2,1)}, bf16[2,128,384]{2,1,0:T(8,128)(2,1)}, f32[2,8,128]{2,1,0:T(8,128)}) custom-call(s32[1,2,4]{2,1,0:T(2,128)} %neighbours_hbm.1, s32[1,2,4]{2,1,0:T(2,128)} %counts_hbm.1, bf16[1,2,128,384]{3,2,1,0:T(8,128)(2,1)} %feat.1, bf16[16,128]{1,0:T(8,128)(2,1)} %bitcast.3, bf16[1,2,128,384]{3,2,1,0:T(8,128)(2,1)} %grad_out.1, ...), custom_call_target="tpu_custom_call" | custom-call | tf_op jit(solution)/shard_map/layer_backward/pallas_call | solution.py:600
  55.8 2.6 %scale_weights.1 = (bf16[1,2,128,384]{3,2,1,0:T(8,128)(2,1)}, f32[1,2,8,128]{3,2,1,0:T(8,128)}, f32[384,384]{1,0:T(8,128)}, f32[384,384]{1,0:T(8,128)}, f32[384,384]{1,0:T(8,128)}, /*index=5*/f32[384,384]{1,0:T(8,128)}) custom-call(bf16[1536,384]{1,0:T(8,128)(2,1)} %bitcast.2, bf16[2,128,384]{2,1,0:T(8,128)(2,1)} %get-tuple-element.10.grad_feat, ...), custom_call_target="tpu_custom_call" | custom-call | tf_op jit(solution)/shard_map/scale_weights/pallas_call | solution.py:685

commit v8 on v7

--- a/solution.py
+++ b/solution.py
@@ -327,6 +327,10 @@
         (neighbours_hbm, neighbours, 5),
         (counts_hbm, counts, 6),
     ]
+    for _, device in plane_peers():
+        greet(device)
+    for _, device in depth_peers():
+        greet(device)
     greet(partner)
     greet(off)
 
@@ -340,13 +344,9 @@
         greet((lat + 1, off_lon))
         greet((lat + 1, partner[1]))
 
+
     for src, dst, index in loads:
         pltpu.make_async_copy(src, dst, local_sem.at[index]).start()
-    for _, device in plane_peers():
-        greet(device)
-    for _, device in depth_peers():
-        greet(device)
-
     near_bias[4] = key_bias[...]
     inner = jnp.minimum(lat, 1) + jnp.minimum(nlat - 1 - lat, 1)
     pl.semaphore_wait(barrier, NPEER + 2 * inner)

time: 58.5 us -> 59.9 us (1.024)
  Pallas kernels: 57.7 us -> 59.1 us
    pallas_call x1, Pallas kernels: 55.1 us -> 56.5 us  [layer_call(): pl.pallas_call(layer_kernel, out_shape=[jax.ShapeDtypeStruct((2 * NPEER,...]
where the time goes in v8:
time: 59.9 us; the launch traced here: 59.7 us
  Pallas kernels  59.1 us (99%)
  between operations  0.64 us (1%)
    pallas_call x1, Pallas kernels, layer_call(): pl.pallas_call(layer_kernel, out_shape=[jax.ShapeDtypeStruct((2 * NPEER,...  56.5 us
    pallas_call x1, Pallas kernels, finish_call(): pl.pallas_call(functools.partial(finish_kernel, scale), out_shape=[jax.Sh...  2.56 us

profile of v8, /device:TPU:1, one launch (start us, length us, event | category | flops | bytes accessed | tf_op | source)
XLA Modules:
  0.0 59.7 jit_solution(12280034722732374819)
XLA Ops:
  0.6 56.5 %layer_backward.1 = (bf16[48,32,384]{2,1,0:T(8,128)(2,1)}, bf16[2,128,384]{2,1,0:T(8,128)(2,1)}, f32[2,8,128]{2,1,0:T(8,128)}) custom-call(s32[1,2,4]{2,1,0:T(2,128)} %neighbours_hbm.1, s32[1,2,4]{2,1,0:T(2,128)} %counts_hbm.1, bf16[1,2,128,384]{3,2,1,0:T(8,128)(2,1)} %feat.1, bf16[16,128]{1,0:T(8,128)(2,1)} %bitcast.3, bf16[1,2,128,384]{3,2,1,0:T(8,128)(2,1)} %grad_out.1, ...), custom_call_target="tpu_custom_call" | custom-call | tf_op jit(solution)/shard_map/layer_backward/pallas_call | solution.py:600
  57.2 2.6 %scale_weights.1 = (bf16[1,2,128,384]{3,2,1,0:T(8,128)(2,1)}, f32[1,2,8,128]{3,2,1,0:T(8,128)}, f32[384,384]{1,0:T(8,128)}, f32[384,384]{1,0:T(8,128)}, f32[384,384]{1,0:T(8,128)}, /*index=5*/f32[384,384]{1,0:T(8,128)}) custom-call(bf16[1536,384]{1,0:T(8,128)(2,1)} %bitcast.2, bf16[2,128,384]{2,1,0:T(8,128)(2,1)} %get-tuple-element.10.grad_feat, ...), custom_call_target="tpu_custom_call" | custom-call | tf_op jit(solution)/shard_map/scale_weights/pallas_call | solution.py:685
